TPU v7x, 32 devices: a whole 2x2x4 slice. The times are simulated.
32 devices in a mesh: facet: 2 (over y), tile: 16 (over z, x, core).
Axes of the slice: x: 2, y: 2, z: 4, core: 2. Of those that a mesh axis runs over, the one named last changes fastest.
Arguments:
- sectioned_rows: bfloat16 [2, 256, 2048], P('facet', 'tile'), may hold values from -6 to 6
- reader: int32 [16, 2], P('tile'), may hold values from 0 to 1, each once within a row
- baseline_coords: float32 [2, 2, 256], P(None, None, 'tile'), may hold values from -8 to 8
- subgrid_index: int32 [2, 256], P(None, 'tile'), may hold values from 0 to 63
- stations: int32 [2, 2, 256], P(None, None, 'tile'), may hold values from 0 to 511
- plane_index: int32 [2, 256], P(None, 'tile'), may hold values from 0 to 31
- model_grid: bfloat16 [2, 64, 2048], P('facet', 'tile'), may hold values from -0.1875 to 0.1875
- beam_screens: bfloat16 [2, 512, 2048], P('facet'), may hold values from -3.5 to 3.5
- plane_phase: float32 [32, 1024], replicated, may hold values from -3.140625 to 3.140625
- channel_freq: float32 [1024], replicated, may hold values from 0.25 to 1.75
Outputs:
- residual: float32 [2, 256, 2048], P('facet', 'tile')
- dirty_grid: float32 [2, 64, 2048], P('facet', 'tile')
Inputs may be any that keep to these rules, and one draw needn't show every extreme that they name: `reader`: for each run of baselines, each facet group read exactly one block.
All inputs are finite; a program needn't handle non-finite values.
Results may differ from a plain program's by a relative error of at most 0.0033.
Values may be sent and summed in bfloat16 or wider, within the bound.
A program may use at most 128 MiB of HBM per device.

v0:
```python
import math

import jax
import jax.numpy as jnp
from jax import lax
from jax.sharding import PartitionSpec as P

TWO_PI = 2.0 * math.pi


def phasor_tables(coords, channel_freq, edge_cells):
    offsets = (jnp.arange(edge_cells, dtype=jnp.float32) - edge_cells // 2) / edge_cells
    angles = TWO_PI * coords[:, None, None] * offsets[None, :, None] * channel_freq[None, None, :]
    return (jnp.cos(angles).astype(jnp.bfloat16), jnp.sin(angles).astype(jnp.bfloat16))


def north_matrix(north_cos, north_sin):
    upper_half = jnp.concatenate([north_cos, north_sin], axis=2)
    lower_half = jnp.concatenate([-north_sin, north_cos], axis=2)
    return jnp.concatenate([upper_half, lower_half], axis=1)


def screen_parts(screens, station_pair, plane_rows, plane_phase):
    pixels = plane_phase.shape[1]
    station_one = screens[station_pair[0]].astype(jnp.float32)
    station_two = screens[station_pair[1]].astype(jnp.float32)
    one_re, one_im = (station_one[:, :pixels], station_one[:, pixels:])
    two_re, two_im = (station_two[:, :pixels], station_two[:, pixels:])
    pair_re = one_re * two_re + one_im * two_im
    pair_im = one_im * two_re - one_re * two_im
    angles = plane_phase[plane_rows]
    wave_re, wave_im = (jnp.cos(angles), jnp.sin(angles))
    return (pair_re * wave_re - pair_im * wave_im, pair_re * wave_im + pair_im * wave_re)


def degrid_rows(model_rows, screen_re, screen_im, east_cos, east_sin, north_mat):
    row_count = model_rows.shape[0]
    pixels = model_rows.shape[1] // 2
    edge_cells = east_cos.shape[1]
    channels = east_cos.shape[2]
    model_f = model_rows.astype(jnp.float32)
    model_re, model_im = (model_f[:, :pixels], model_f[:, pixels:])
    image_re = screen_re * model_re - screen_im * model_im
    image_im = screen_re * model_im + screen_im * model_re
    operand = jnp.concatenate(
        [
            image_re.reshape(row_count, edge_cells, edge_cells),
            image_im.reshape(row_count, edge_cells, edge_cells),
        ],
        axis=2,
    ).astype(jnp.bfloat16)
    inner_sum = jnp.einsum("rxy,ryc->rxc", operand, north_mat, preferred_element_type=jnp.float32)
    inner_re, inner_im = (inner_sum[:, :, :channels], inner_sum[:, :, channels:])
    cos_f, sin_f = (east_cos.astype(jnp.float32), east_sin.astype(jnp.float32))
    vis_re = jnp.sum(cos_f * inner_re - sin_f * inner_im, axis=1)
    vis_im = jnp.sum(cos_f * inner_im + sin_f * inner_re, axis=1)
    return jnp.concatenate([vis_re, vis_im], axis=1)


def grid_rows(resid_rows, screen_re, screen_im, east_cos, east_sin, north_mat, grid_scale):
    row_count = resid_rows.shape[0]
    edge_cells = east_cos.shape[1]
    channels = east_cos.shape[2]
    resid_re, resid_im = (resid_rows[:, None, :channels], resid_rows[:, None, channels:])
    cos_f, sin_f = (east_cos.astype(jnp.float32), east_sin.astype(jnp.float32))
    weighted_re = cos_f * resid_re + sin_f * resid_im
    weighted_im = cos_f * resid_im - sin_f * resid_re
    operand = jnp.concatenate([weighted_re, weighted_im], axis=2).astype(jnp.bfloat16)
    gridded = jnp.einsum("rxc,ryc->rxy", operand, north_mat, preferred_element_type=jnp.float32)
    grid_re = gridded[:, :, :edge_cells].reshape(row_count, edge_cells * edge_cells)
    grid_im = gridded[:, :, edge_cells:].reshape(row_count, edge_cells * edge_cells)
    out_re = (screen_re * grid_re + screen_im * grid_im) * grid_scale
    out_im = (screen_re * grid_im - screen_im * grid_re) * grid_scale
    return jnp.concatenate([out_re, out_im], axis=1).astype(jnp.bfloat16)


def local(
    sectioned_rows,
    reader,
    baseline_coords,
    subgrid_index,
    stations,
    plane_index,
    model_grid,
    beam_screens,
    plane_phase,
    channel_freq,
):
    n_facet = lax.axis_size("facet")
    n_tile = lax.axis_size("tile")
    facet_id = lax.axis_index("facet")
    channels = channel_freq.shape[0]
    pixels = plane_phase.shape[1]
    edge_cells = math.isqrt(pixels)
    row_block = sectioned_rows.shape[1]
    owned = model_grid.shape[1]
    subgrid_count = owned * n_tile
    grid_scale = 1.0 / math.sqrt(channels * n_facet * (row_block * n_tile) / subgrid_count)
    arrived = lax.all_gather(sectioned_rows, "facet", axis=0, tiled=True)
    visible = jnp.take(arrived, reader[0], axis=0)
    model_all = lax.all_gather(model_grid, "tile", axis=1, tiled=True)[0]
    screens_own = beam_screens[0]
    block_ids = jnp.arange(n_facet, dtype=jnp.int32)

    def geometry(block_id):
        east_cos, east_sin = phasor_tables(baseline_coords[block_id, 0], channel_freq, edge_cells)
        north_cos, north_sin = phasor_tables(baseline_coords[block_id, 1], channel_freq, edge_cells)
        screen_re, screen_im = screen_parts(
            screens_own, stations[block_id], plane_index[block_id], plane_phase
        )
        return (east_cos, east_sin, north_matrix(north_cos, north_sin), screen_re, screen_im)

    tables = lax.map(geometry, block_ids)

    def predict(inputs):
        rows_sub, east_cos, east_sin, north_mat, screen_re, screen_im = inputs
        return degrid_rows(model_all[rows_sub], screen_re, screen_im, east_cos, east_sin, north_mat)

    predicted = lax.map(predict, (subgrid_index,) + tuple(tables))
    total = lax.psum(predicted, "facet")
    resid_all = visible.astype(jnp.float32) - total
    mine = lax.dynamic_index_in_dim(resid_all, facet_id, 0, keepdims=True)

    def regrid(inputs):
        resid_block, east_cos, east_sin, north_mat, screen_re, screen_im = inputs
        return grid_rows(
            resid_block, screen_re, screen_im, east_cos, east_sin, north_mat, grid_scale
        )

    regridded = lax.map(regrid, (resid_all,) + tuple(tables)).reshape(
        n_facet * row_block, 2 * pixels
    )
    targets = subgrid_index.reshape(-1)
    onehot = (jnp.arange(subgrid_count, dtype=jnp.int32)[:, None] == targets[None, :]).astype(
        jnp.bfloat16
    )
    partial_sums = jnp.dot(onehot, regridded, preferred_element_type=jnp.float32)
    dirty = lax.psum_scatter(partial_sums, "tile", scatter_dimension=0, tiled=True)
    return (mine, dirty[None])


def solution(mesh):
    return jax.shard_map(
        local,
        mesh=mesh,
        in_specs=(
            P("facet", "tile", None),
            P("tile", None),
            P(None, None, "tile"),
            P(None, "tile"),
            P(None, None, "tile"),
            P(None, "tile"),
            P("facet", "tile", None),
            P("facet", None, None),
            P(),
            P(),
        ),
        out_specs=(P("facet", "tile", None), P("facet", "tile", None)),
        check_vma=False,
    )
```

profile of v0, /device:TPU:0, one launch (start us, length us, event | category | flops | bytes accessed | tf_op | source)
XLA Modules:
  0.0 251.1 jit_solution(4339849306536953310)
XLA Ops:
  7.3 74.6 %while.40 = (s32[]{:T(128)}, bf16[2,16,32,1024]{3,2,1,0:T(8,128)(2,1)S(1)}, bf16[2,16,32,1024]{3,2,1,0:T(8,128)(2,1)}, bf16[2,16,64,2048]{3,2,1,0:T(8,128)(2,1)}...) while((s32[]{:T(128)}, ...), condition=%wide.region_1.2_spmd, body=%wide.region_0.1_spmd.sunk | while | flops 22810868 | bytes 31846404 | solution.py:113
  10.4 8.7 %fusion.76 = (bf16[16,32,1024]{2,1,0:T(8,128)(2,1)S(1)}, bf16[16,32,1024]{2,1,0:T(8,128)(2,1)S(1)}) fusion(f32[1024]{0:T(1024)} %get-tuple-element.630, f32[16,32]{1,0:T(8,128)S(1)} %get-tuple-element.550), kind=kLoop, calls=%fused_computation.34.clone.2 | loop fusion | flops 1572864 | bytes 2103296 | tf_op jit(solution)/shard_map/while/body/eval_jaxpr/convert_element_type | solution.py:14
  19.2 7.2 %fusion.77 = bf16[16,32,1024]{2,1,0:T(8,128)(2,1)S(1)} fusion(f32[1024]{0:T(1024)S(1)} %copy-done.4, f32[16,32]{1,0:T(8,128)S(1)} %get-tuple-element.550), kind=kLoop, calls=%fused_computation.37.clone.1 | loop fusion | flops 2621440 | bytes 1054720 | tf_op jit(solution)/shard_map/while/body/eval_jaxpr/neg | solution.py:19
  26.4 2.1 fusion.78
  29.1 8.1 %fusion.75 = (bf16[2,16,32,1024]{3,2,1,0:T(8,128)(2,1)S(1)}, bf16[2,16,32,1024]{3,2,1,0:T(8,128)(2,1)S(1)}) fusion(bf16[2,16,32,1024]{3,2,1,0:T(8,128)(2,1)S(1)} %copy-done, s32[]{:T(128)} %get-tuple-element.606, f32[1024]{0:T(1024)S(1)} %copy-done.4, f32[16,32]{1,0:T(8,128)S(1)} %get-tuple-element.547, ...), kind=kLoop, calls=%fused_computation.35.clone.1 | loop fusion | flops 1572864 | bytes 2109444 | tf_op jit(solution)/shard_map/while/body/jit(dynamic_update_index_in_dim)/dynamic_update_slice | solution.py:113
  37.2 1.4 copy-done.1
  39.4 2.5 %gather_fusion.1 = bf16[16,2048]{1,0:T(8,128)(2,1)S(1)} fusion(bf16[512,2048]{1,0:T(8,128)(2,1)} %get-tuple-element.632, s32[1024]{0:T(1024)S(1)} %pad_clamp_fusion.10), kind=kCustom, calls=%fused_computation.1.clone.1 | custom fusion | bytes 131136 | tf_op jit(solution)/shard_map/while/body/eval_jaxpr/gather | solution.py:26
  42.0 2.5 %gather_fusion.2 = bf16[16,2048]{1,0:T(8,128)(2,1)S(1)} fusion(bf16[512,2048]{1,0:T(8,128)(2,1)} %get-tuple-element.632, s32[1024]{0:T(1024)S(1)} %pad_clamp_fusion.11), kind=kCustom, calls=%fused_computation.clone.1 | custom fusion | bytes 131136 | tf_op jit(solution)/shard_map/while/body/eval_jaxpr/gather | solution.py:25
  47.7 8.7 %fusion.76 = (bf16[16,32,1024]{2,1,0:T(8,128)(2,1)S(1)}, bf16[16,32,1024]{2,1,0:T(8,128)(2,1)S(1)}) fusion(f32[1024]{0:T(1024)} %get-tuple-element.630, f32[16,32]{1,0:T(8,128)S(1)} %get-tuple-element.550), kind=kLoop, calls=%fused_computation.34.clone.2 | loop fusion | flops 1572864 | bytes 2103296 | tf_op jit(solution)/shard_map/while/body/eval_jaxpr/convert_element_type | solution.py:14
  56.5 7.2 %fusion.77 = bf16[16,32,1024]{2,1,0:T(8,128)(2,1)S(1)} fusion(f32[1024]{0:T(1024)S(1)} %copy-done.4, f32[16,32]{1,0:T(8,128)S(1)} %get-tuple-element.550), kind=kLoop, calls=%fused_computation.37.clone.1 | loop fusion | flops 2621440 | bytes 1054720 | tf_op jit(solution)/shard_map/while/body/eval_jaxpr/neg | solution.py:19
  63.7 2.2 fusion.78
  66.4 8.1 %fusion.75 = (bf16[2,16,32,1024]{3,2,1,0:T(8,128)(2,1)S(1)}, bf16[2,16,32,1024]{3,2,1,0:T(8,128)(2,1)S(1)}) fusion(bf16[2,16,32,1024]{3,2,1,0:T(8,128)(2,1)S(1)} %copy-done, s32[]{:T(128)} %get-tuple-element.606, f32[1024]{0:T(1024)S(1)} %copy-done.4, f32[16,32]{1,0:T(8,128)S(1)} %get-tuple-element.547, ...), kind=kLoop, calls=%fused_computation.35.clone.1 | loop fusion | flops 1572864 | bytes 2109444 | tf_op jit(solution)/shard_map/while/body/jit(dynamic_update_index_in_dim)/dynamic_update_slice | solution.py:113
  74.5 1.4 copy-done.1
  76.7 2.5 %gather_fusion.1 = bf16[16,2048]{1,0:T(8,128)(2,1)S(1)} fusion(bf16[512,2048]{1,0:T(8,128)(2,1)} %get-tuple-element.632, s32[1024]{0:T(1024)S(1)} %pad_clamp_fusion.10), kind=kCustom, calls=%fused_computation.1.clone.1 | custom fusion | bytes 131136 | tf_op jit(solution)/shard_map/while/body/eval_jaxpr/gather | solution.py:26
  79.3 2.5 %gather_fusion.2 = bf16[16,2048]{1,0:T(8,128)(2,1)S(1)} fusion(bf16[512,2048]{1,0:T(8,128)(2,1)} %get-tuple-element.632, s32[1024]{0:T(1024)S(1)} %pad_clamp_fusion.11), kind=kCustom, calls=%fused_computation.clone.1 | custom fusion | bytes 131136 | tf_op jit(solution)/shard_map/while/body/eval_jaxpr/gather | solution.py:25
  82.0 24.6 %all_gather.7 = bf16[1,64,2048]{2,0,1:T(2,128)(2,1)S(1)} all-gather(bf16[1,4,2048]{2,0,1:T(2,128)(2,1)S(1)} %copy.13), channel_id=1, replica_groups=mesh['facet'=2,'tile'=16] {'tile'}, dimensions={1}, use_global_device_ids=true | all-gather | bytes 278528 | tf_op jit(solution)/shard_map/all_gather | solution.py:101
  106.7 10.4 %while.41 = (s32[]{:T(128)}, f32[2,16,2048]{2,1,0:T(8,128)S(1)}, bf16[2,16,32,1024]{3,2,1,0:T(8,128)(2,1)S(1)}, f32[2,16,1024]{2,1,0:T(8,128)S(1)}, s32[2,16]{1,...) while((s32[]{:T(128)}, f32[2,16,2048]{2,1,0:T(8,128)S(1)}, ...), condition=%wide.region_5.6_spmd, body=%wide.region_2.5_spmd.sunk | while | flops 139756592 | bytes 24318864 | solution.py:119
  107.7 3.1 %fusion.85 = f32[16,32,2048]{2,1,0:T(8,128)S(1)} fusion(bf16[2,16,64,2048]{3,2,1,0:T(8,128)(2,1)} %get-tuple-element.665, s32[]{:T(128)} %get-tuple-element.648, bf16[16,32,32]{2,1,0:T(8,128)(2,1)S(1)} %reshape.407, bf16[16,32,32]{2,1,0:T(8,128)(2,1)S(1)} %reshape.408), kind=kOutput, calls=%fused_computation.63.clone.1 | convolution fusion | flops 134348800 | bytes 8454656 | tf_op jit(solution)/shard_map/while/body/eval_jaxpr/rxy,ryc->rxc/dot_general | solution.py:52
  110.9 1.0 fusion.86
  112.9 3.1 %fusion.85 = f32[16,32,2048]{2,1,0:T(8,128)S(1)} fusion(bf16[2,16,64,2048]{3,2,1,0:T(8,128)(2,1)} %get-tuple-element.665, s32[]{:T(128)} %get-tuple-element.648, bf16[16,32,32]{2,1,0:T(8,128)(2,1)S(1)} %reshape.407, bf16[16,32,32]{2,1,0:T(8,128)(2,1)S(1)} %reshape.408), kind=kOutput, calls=%fused_computation.63.clone.1 | convolution fusion | flops 134348800 | bytes 8454656 | tf_op jit(solution)/shard_map/while/body/eval_jaxpr/rxy,ryc->rxc/dot_general | solution.py:52
  116.1 1.0 fusion.86
  118.0 5.7 %all_gather.6 = bf16[2,16,2048]{2,1,0:T(8,128)(2,1)S(1)} all-gather(bf16[1,16,2048]{2,1,0:T(8,128)(2,1)S(1)} %copy-done.6), channel_id=1, replica_groups=mesh['facet'=2,'tile'=16] {'facet'}, dimensions={0}, use_global_device_ids=true | all-gather | bytes 196608 | tf_op jit(solution)/shard_map/all_gather | solution.py:99
  124.3 14.2 %all-reduce.4.cloned.1.call-done = f32[2,16,2048]{2,1,0:T(8,128)} async-done(((f32[2,16,2048]{2,1,0:T(8,128)}), f32[2,16,2048]{2,1,0:T(8,128)}) %all-reduce.4.cloned.1.call-update) | async-done | bytes 262160 | tf_op jit(solution)/shard_map/psum | solution.py:120
  138.5 1.0 convert_subtract_fusion
  139.6 11.9 %while.42 = (s32[]{:T(128)}, bf16[2,16,2048]{2,1,0:T(8,128)(2,1)S(1)}, f32[2,16,1024]{2,1,0:T(8,128)S(1)}, bf16[2,16,32,1024]{3,2,1,0:T(8,128)(2,1)S(1)}, f32[2,...) while((s32[]{:T(128)}, ...), condition=%wide.region_8.9_spmd, body=%wide.region_7.8_spmd.sunk | while | flops 143949824 | bytes 12255853 | solution.py:130
  139.6 2.0 fusion.91
  141.6 3.4 %fusion.92 = f32[16,32,64]{2,1,0:T(8,128)S(1)} fusion(bf16[2,16,64,2048]{3,2,1,0:T(8,128)(2,1)} %get-tuple-element.692, s32[]{:T(128)} %get-tuple-element.677, bf16[16,32,1024]{2,1,0:T(8,128)(2,1)S(1)} %get-tuple-element.584, bf16[16,32,1024]{2,1,0:T(8,128)(2,1)S(1)} %get-tuple-element.585), kind=kOutput, calls=%fused_computation.5.clone.1 | convolution fusion | flops 138412032 | bytes 6423040 | tf_op jit(solution)/shard_map/while/body/eval_jaxpr/rxc,ryc->rxy/dot_general | solution.py:69
  145.6 2.0 fusion.91
  147.6 3.4 %fusion.92 = f32[16,32,64]{2,1,0:T(8,128)S(1)} fusion(bf16[2,16,64,2048]{3,2,1,0:T(8,128)(2,1)} %get-tuple-element.692, s32[]{:T(128)} %get-tuple-element.677, bf16[16,32,1024]{2,1,0:T(8,128)(2,1)S(1)} %get-tuple-element.584, bf16[16,32,1024]{2,1,0:T(8,128)(2,1)S(1)} %get-tuple-element.585), kind=kOutput, calls=%fused_computation.5.clone.1 | convolution fusion | flops 138412032 | bytes 6423040 | tf_op jit(solution)/shard_map/while/body/eval_jaxpr/rxc,ryc->rxy/dot_general | solution.py:69
  151.5 1.0 fusion.47
  154.5 88.3 %all-reduce.6.cloned.1.call-done = f32[64,2048]{1,0:T(8,128)} async-done(((f32[64,2048]{1,0:T(8,128)}), f32[64,2048]{1,0:T(8,128)}) %all-reduce.6.cloned.1.call-update) | async-done | bytes 524304
  242.8 1.5 dynamic-slice_bitcast_fusion.1
  (119 shorter events, 11.7 us)
Async XLA Ops:
  7.2 131.4 %all-reduce.4.cloned.1.call-start = ((), (), s32[]{:S(2)}) async-start(), calls=%async_computation | async-start | bytes 524288 | tf_op jit(solution)/shard_map/psum | solution.py:120
  7.3 74.6 %copy-start.7 = (bf16[1,4,2048]{2,1,0:T(4,128)(2,1)S(1)}, bf16[1,4,2048]{2,1,0:T(4,128)(2,1)}, u32[]{:S(2)}) copy-start(bf16[1,4,2048]{2,1,0:T(4,128)(2,1)} %param.22) | copy-start | bytes 49156
  7.3 99.4 %copy-start.10 = (s32[2,16]{1,0:T(2,128)S(1)}, s32[2,16]{1,0:T(2,128)}, u32[]{:S(2)}) copy-start(s32[2,16]{1,0:T(2,128)} %param.19) | copy-start | bytes 388
  7.3 11.9 %copy-start.4 = (f32[1024]{0:T(1024)S(1)}, f32[1024]{0:T(1024)}, u32[]{:S(2)}) copy-start(f32[1024]{0:T(1024)} %get-tuple-element.630) | copy-start | bytes 12292 | tf_op jit(solution)/shard_map/while
  26.4 2.7 %copy-start = (bf16[2,16,32,1024]{3,2,1,0:T(8,128)(2,1)S(1)}, bf16[2,16,32,1024]{3,2,1,0:T(8,128)(2,1)}, u32[]{:S(2)}) copy-start(bf16[2,16,32,1024]{3,2,1,0:T(8,128)(2,1)} %get-tuple-element.608) | copy-start | bytes 6291460 | tf_op jit(solution)/shard_map/while
  28.5 10.0 %copy-start.8 = (s32[2,2,16]{2,1,0:T(2,128)S(1)}, s32[2,2,16]{2,1,0:T(2,128)}, u32[]{:S(2)}) copy-start(s32[2,2,16]{2,1,0:T(2,128)} %get-tuple-element.631) | copy-start | bytes 772 | tf_op jit(solution)/shard_map/while
  28.5 10.0 %copy-start.9 = (s32[2,16]{1,0:T(2,128)S(1)}, s32[2,16]{1,0:T(2,128)}, u32[]{:S(2)}) copy-start(s32[2,16]{1,0:T(2,128)} %get-tuple-element.633) | copy-start | bytes 388 | tf_op jit(solution)/shard_map/while
  28.5 10.1 %copy-start.3 = (f32[32,1024]{1,0:T(8,128)S(1)}, f32[32,1024]{1,0:T(8,128)}, u32[]{:S(2)}) copy-start(f32[32,1024]{1,0:T(8,128)} %get-tuple-element.634) | copy-start | bytes 393220 | tf_op jit(solution)/shard_map/while
  37.1 1.4 copy-start.1
  44.6 11.9 %copy-start.4 = (f32[1024]{0:T(1024)S(1)}, f32[1024]{0:T(1024)}, u32[]{:S(2)}) copy-start(f32[1024]{0:T(1024)} %get-tuple-element.630) | copy-start | bytes 12292 | tf_op jit(solution)/shard_map/while
  63.7 2.7 %copy-start = (bf16[2,16,32,1024]{3,2,1,0:T(8,128)(2,1)S(1)}, bf16[2,16,32,1024]{3,2,1,0:T(8,128)(2,1)}, u32[]{:S(2)}) copy-start(bf16[2,16,32,1024]{3,2,1,0:T(8,128)(2,1)} %get-tuple-element.608) | copy-start | bytes 6291460 | tf_op jit(solution)/shard_map/while
  65.9 10.0 %copy-start.8 = (s32[2,2,16]{2,1,0:T(2,128)S(1)}, s32[2,2,16]{2,1,0:T(2,128)}, u32[]{:S(2)}) copy-start(s32[2,2,16]{2,1,0:T(2,128)} %get-tuple-element.631) | copy-start | bytes 772 | tf_op jit(solution)/shard_map/while
  65.9 10.0 %copy-start.9 = (s32[2,16]{1,0:T(2,128)S(1)}, s32[2,16]{1,0:T(2,128)}, u32[]{:S(2)}) copy-start(s32[2,16]{1,0:T(2,128)} %get-tuple-element.633) | copy-start | bytes 388 | tf_op jit(solution)/shard_map/while
  65.9 10.0 %copy-start.3 = (f32[32,1024]{1,0:T(8,128)S(1)}, f32[32,1024]{1,0:T(8,128)}, u32[]{:S(2)}) copy-start(f32[32,1024]{1,0:T(8,128)} %get-tuple-element.634) | copy-start | bytes 393220 | tf_op jit(solution)/shard_map/while
  74.4 1.4 copy-start.1
  106.7 11.2 %copy-start.11 = (s32[1,2]{1,0:T(1,128)S(1)}, s32[1,2]{1,0:T(1,128)}, u32[]{:S(2)}) copy-start(s32[1,2]{1,0:T(1,128)} %param.17) | copy-start | bytes 28
  106.7 11.3 %copy-start.6 = (bf16[1,16,2048]{2,1,0:T(8,128)(2,1)S(1)}, bf16[1,16,2048]{2,1,0:T(8,128)(2,1)}, u32[]{:S(2)}) copy-start(bf16[1,16,2048]{2,1,0:T(8,128)(2,1)} %param.16) | copy-start | bytes 196612
  107.7 3.1 %copy-start.2 = (bf16[2,16,32,1024]{3,2,1,0:T(8,128)(2,1)S(1)}, bf16[2,16,32,1024]{3,2,1,0:T(8,128)(2,1)}, u32[]{:S(2)}) copy-start(bf16[2,16,32,1024]{3,2,1,0:T(8,128)(2,1)} %get-tuple-element.666) | copy-start | bytes 6291460 | tf_op jit(solution)/shard_map/while
  112.9 3.1 %copy-start.2 = (bf16[2,16,32,1024]{3,2,1,0:T(8,128)(2,1)S(1)}, bf16[2,16,32,1024]{3,2,1,0:T(8,128)(2,1)}, u32[]{:S(2)}) copy-start(bf16[2,16,32,1024]{3,2,1,0:T(8,128)(2,1)} %get-tuple-element.666) | copy-start | bytes 6291460 | tf_op jit(solution)/shard_map/while
  117.1 0.7 copy-start.5
  117.9 124.9 %all-reduce.6.cloned.1.call-start = ((), (), s32[]{:S(2)}) async-start(), calls=%async_computation.1 | async-start | bytes 1048576
  139.6 13.0 %copy-start.12 = (u32[32]{0:T(128)S(1)}, u32[32]{0:T(128)}, u32[]{:S(2)}) copy-start(u32[32]{0:T(128)} %constant.133) | copy-start | bytes 388
Sparse Core Ops, SparseCore 0:
  118.0 20.4 all-reduce.3
  152.7 90.0 all-reduce.5
where the time goes:
time: 252 us; the launch traced here: 251 us
  waiting for transfers between devices  103 us (41%)
  other arithmetic  61.5 us (24%)
  blocking collectives  30.3 us (12%)
  local copies, waits for them, and re-layouts  23.8 us (9%)
  between operations  14.9 us (6%)
  matrix products  14 us (6%)
  loops' own time  4 us (2%)
    unnamed x3, waiting for transfers between devices  88.3 us
    all_gather x1, blocking collectives, local(): model_all = lax.all_gather(model_grid, 'tile', axis=1, tiled=True)[0]  24.6 us
    dynamic_update_slice x8, other arithmetic, local(): tables = lax.map(geometry, block_ids)  20.5 us
    convert_element_type x2, other arithmetic, phasor_tables(): jnp.sin(angles).astype(jnp.bfloat16)  17.4 us
    neg x2, other arithmetic, north_matrix(): lower_half = jnp.concatenate([-north_sin, north_cos], axis=2)  14.4 us
    psum x1, waiting for transfers between devices, local(): total = lax.psum(predicted, 'facet')  14.2 us
    dot_general x2, matrix products, grid_rows(): jnp.einsum('rxc,ryc->rxy', operand, north_mat, preferred_element_type=jnp...  6.82 us
    dot_general x2, matrix products, degrid_rows(): jnp.einsum('rxy,ryc->rxc', operand, north_mat, preferred_element_type=jnp...  6.22 us
  transfers between devices with their start and end apart: 2, of which 2 were waited for; matrix products, arithmetic and copies ran while one was open for 1% of the time, Pallas kernels for 0%

commit v1 on v0

v1 whole, which is shorter than its diff:
```python
import functools
import math

import jax
import jax.numpy as jnp
from jax import lax
from jax.experimental import pallas as pl
from jax.experimental.pallas import tpu as pltpu
from jax.sharding import PartitionSpec as P

MESH = pl.DeviceIdType.MESH
F32 = jnp.float32
BF16 = jnp.bfloat16


def cos_sin(x):
    y = x * x
    c = 1.0 / math.factorial(12)
    s = 1.0 / math.factorial(13)
    for k in range(5, -1, -1):
        sign = -1.0 if k % 2 else 1.0
        c = c * y + sign / math.factorial(2 * k)
        s = s * y + sign / math.factorial(2 * k + 1)
    return c, s * x


def iota(shape, dim):
    return lax.broadcasted_iota(jnp.int32, shape, dim)


def fold_values(cell, part_col):
    k = part_col % 16
    odd = part_col // 16
    hit = (cell == 16 + k).astype(F32)
    other = (cell == 15 - k).astype(F32)
    value = hit + other * (1.0 - 2.0 * odd.astype(F32))
    return jnp.where(part_col < 32, value, 0.0).astype(BF16)


def kernel(
    n_facet, n_tile, owned, run, channels, grid_scale,
    reader_ref, cols_ref, index_ref, index_col_ref, index_row_ref,
    rows_ref, model_ref, screens_hbm, phase_ref, freq_ref,
    resid_ref, dirty_ref,
    screens, model_send, model_all, arrived, pred_send, pred_all, part_send, part_all,
    te, tn, mats, hre, him, vre, vim, sre, sim,
    local_sem, model_ss, model_rs, vis_ss, vis_rs, pred_ss, pred_rs, part_ss, part_rs,
):
    R = n_facet * run
    me_f = lax.axis_index("facet")
    me_t = lax.axis_index("tile")
    chunk = model_send.shape[0]
    quarter = model_send.shape[1]

    load = pltpu.make_async_copy(screens_hbm, screens, local_sem)
    load.start()

    def tile_peer(p):
        return lax.rem(me_t + p, n_tile)

    def facet_peer(p):
        return lax.rem(me_f + p, n_facet)

    barrier = pltpu.get_barrier_semaphore()

    def greet_tile(p, c):
        pl.semaphore_signal(barrier, inc=1, device_id=(me_f, tile_peer(p)), device_id_type=MESH)
        return c

    def greet_facet(p, c):
        pl.semaphore_signal(barrier, inc=1, device_id=(facet_peer(p), me_t), device_id_type=MESH)
        return c

    lax.fori_loop(1, n_tile, greet_tile, 0)
    lax.fori_loop(1, n_facet, greet_facet, 0)

    model_f = model_ref[0].astype(F32)
    model_send[...] = jnp.concatenate(
        [model_f[:, q * quarter:(q + 1) * quarter] for q in range(4)], axis=0
    ).astype(BF16)
    pl.semaphore_wait(barrier, n_tile + n_facet - 2)

    def model_copy(o, slot):
        return pltpu.make_async_remote_copy(
            src_ref=model_send, dst_ref=model_all.at[slot], send_sem=model_ss.at[o],
            recv_sem=model_rs.at[slot], device_id=(me_f, o), device_id_type=MESH)

    def vis_copy(o, slot):
        return pltpu.make_async_remote_copy(
            src_ref=rows_ref.at[0], dst_ref=arrived.at[slot], send_sem=vis_ss.at[o],
            recv_sem=vis_rs.at[slot], device_id=(o, me_t), device_id_type=MESH)

    def pred_copy(o, slot, k):
        return pltpu.make_async_remote_copy(
            src_ref=pred_send.at[k], dst_ref=pred_all.at[slot, k], send_sem=pred_ss.at[o, k],
            recv_sem=pred_rs.at[slot, k], device_id=(o, me_t), device_id_type=MESH)

    def part_copy(o, slot):
        return pltpu.make_async_remote_copy(
            src_ref=part_send.at[o], dst_ref=part_all.at[slot], send_sem=part_ss.at[o],
            recv_sem=part_rs.at[slot], device_id=(me_f, o), device_id_type=MESH)

    def send_model(p, c):
        model_copy(tile_peer(p), me_t).start()
        return c

    def send_vis(p, c):
        vis_copy(facet_peer(p), me_f).start()
        return c

    lax.fori_loop(1, n_tile, send_model, 0)
    lax.fori_loop(1, n_facet, send_vis, 0)
    model_all[me_t] = model_send[...]
    arrived[me_f] = rows_ref[0]

    def tables(g, c):
        r0 = pl.multiple_of(g * 8, 8)
        freq = freq_ref[...]
        halves = []
        for col, dst in ((0, te), (1, tn)):
            u = cols_ref[pl.ds(r0, 8), col:col + 1]
            alpha = (u * (2.0 * math.pi / 64.0)) * freq
            c0, s0 = cos_sin(alpha)
            halves.append((c0, s0))
            twice = 2.0 - 4.0 * s0 * s0
            c_old, s_old, c_now, s_now = c0, -s0, c0, s0
            for j in range(16):
                for b in range(channels // 128):
                    lanes = slice(128 * b, 128 * b + 128)
                    dst[b, pl.ds(r0 * 32 + j, 8, stride=32), :] = c_now[:, lanes]
                    dst[b, pl.ds(r0 * 32 + 16 + j, 8, stride=32), :] = s_now[:, lanes]
                if j < 15:
                    c_old, c_now = c_now, twice * c_now - c_old
                    s_old, s_now = s_now, twice * s_now - s_old
        (ca, sa), (cb, sb) = halves
        hre[pl.ds(r0, 8), :] = ca * cb - sa * sb
        him[pl.ds(r0, 8), :] = ca * sb + sa * cb
        return c

    lax.fori_loop(0, R // 8, tables, 0)

    stations = screens.shape[0]
    planes, pixels = phase_ref.shape
    half_c, half_s = cos_sin(phase_ref[...] * 0.5)
    waves = jnp.concatenate([1.0 - 2.0 * half_s * half_s, 2.0 * half_s * half_c], axis=1)
    plane_hot = (index_ref[:, 2:3] == iota((R, planes), 1)).astype(F32)
    wave = jnp.dot(plane_hot, waves, preferred_element_type=F32, precision=lax.Precision.HIGHEST)
    wave_re, wave_im = wave[:, :pixels], wave[:, pixels:]
    load.wait()
    one_hot = (index_ref[:, 0:1] == iota((R, stations), 1)).astype(F32).astype(BF16)
    two_hot = (index_ref[:, 1:2] == iota((R, stations), 1)).astype(F32).astype(BF16)
    one = jnp.dot(one_hot, screens[...], preferred_element_type=F32)
    two = jnp.dot(two_hot, screens[...], preferred_element_type=F32)
    one_re, one_im, two_re, two_im = one[:, :pixels], one[:, pixels:], two[:, :pixels], two[:, pixels:]
    pair_re = one_re * two_re + one_im * two_im
    pair_im = one_im * two_re - one_re * two_im
    sre[...] = pair_re * wave_re - pair_im * wave_im
    sim[...] = pair_re * wave_im + pair_im * wave_re

    def wait_model(p, c):
        o = tile_peer(p)
        model_copy(o, o).wait()
        return c

    lax.fori_loop(1, n_tile, wait_model, 0)
    total = n_tile * chunk
    own_i = iota((4 * R, total), 1)
    pick = (index_col_ref[...] == (own_i // chunk) * owned + own_i % owned) & (
        (own_i // owned) % 4 == iota((4 * R, total), 0) // R)
    found = jnp.dot(pick.astype(F32).astype(BF16), model_all[...].reshape(total, quarter),
                    preferred_element_type=F32)
    model_re = jnp.concatenate([found[:R], found[R:2 * R]], axis=1)
    model_im = jnp.concatenate([found[2 * R:3 * R], found[3 * R:]], axis=1)
    image = jnp.concatenate(
        [sre[...] * model_re - sim[...] * model_im, sre[...] * model_im + sim[...] * model_re], axis=0
    ).astype(BF16)

    fr, fc = iota((128, 512), 0), iota((128, 512), 1)
    fold = jnp.where(fr // 32 == fc // 128, fold_values(fr % 32, fc % 128).astype(F32), 0.0).astype(BF16)
    low = iota((R, 128), 1) < 16
    by_x = {}
    for g in range(8):
        got = jnp.dot(image[:, 128 * g:128 * g + 128], fold, preferred_element_type=F32)
        for i in range(4):
            by_x[4 * g + i] = got[:, 128 * i:128 * i + 128]
    for j in range(16):
        up, down = by_x[16 + j], by_x[15 - j]
        even, odd = up + down, up - down
        e_re, e_im, o_re, o_im = even[:R], even[R:], odd[:R], odd[R:]
        parts = (jnp.where(low, e_re, -e_im), -jnp.where(low, o_im, o_re),
                 jnp.where(low, e_im, e_re), jnp.where(low, o_re, -o_im))
        for q in range(4):
            mats[(q * 16 + j) * R:(q * 16 + j + 1) * R, :] = parts[q]

    step = 256

    def table(ref, at, lo):
        return jnp.concatenate([ref[lo // 128 + b, pl.ds(at, 32), :] for b in range(step // 128)], axis=1)

    def degrid(r):
        lhs = mats[pl.ds(r, 64, stride=R), :][:, :32].astype(BF16)
        at = pl.multiple_of(r * 32, 32)
        for lo in range(0, channels, step):
            inner = jnp.dot(lhs, table(tn, at, lo).astype(BF16), preferred_element_type=F32)
            east = table(te, at, lo)
            vre[pl.ds(r, 1), lo:lo + step] = jnp.sum(east * inner[:32], axis=0, keepdims=True)
            vim[pl.ds(r, 1), lo:lo + step] = jnp.sum(east * inner[32:], axis=0, keepdims=True)

    def predict(k, c):
        def pair(i, d):
            degrid(k * run + 2 * i)
            degrid(k * run + 2 * i + 1)
            return d

        lax.fori_loop(0, run // 2, pair, 0)
        r0 = pl.multiple_of(k * run, run)
        a_re, a_im = vre[pl.ds(r0, run), :], vim[pl.ds(r0, run), :]
        h_re, h_im = hre[pl.ds(r0, run), :], him[pl.ds(r0, run), :]
        p_re = a_re * h_re + a_im * h_im
        p_im = a_im * h_re - a_re * h_im
        vre[pl.ds(r0, run), :] = p_re
        vim[pl.ds(r0, run), :] = p_im
        pred_send[k, :, :channels] = p_re.astype(BF16)
        pred_send[k, :, channels:] = p_im.astype(BF16)

        def send_pred(p, d):
            pred_copy(facet_peer(p), me_f, k).start()
            return d

        lax.fori_loop(1, n_facet, send_pred, 0)
        return c

    lax.fori_loop(0, n_facet, predict, 0)

    def wait_vis(p, c):
        o = facet_peer(p)
        vis_copy(o, o).wait()
        return c

    lax.fori_loop(1, n_facet, wait_vis, 0)

    def regrid(r):
        at = pl.multiple_of(r * 32, 32)
        acc = jnp.zeros((64, 32), F32)
        for lo in range(0, channels, step):
            east = table(te, at, lo)
            weighted = jnp.concatenate(
                [east * vre[pl.ds(r, 1), lo:lo + step], east * vim[pl.ds(r, 1), lo:lo + step]], axis=0
            ).astype(BF16)
            acc = acc + lax.dot_general(
                weighted, table(tn, at, lo).astype(BF16),
                (((1,), (1,)), ((), ())), preferred_element_type=F32)
        mats[pl.ds(r, 64, stride=R), :] = jnp.concatenate([acc, jnp.zeros((64, 96), F32)], axis=1)

    def grid_block(k, c):
        r0 = pl.multiple_of(k * run, run)

        def wait_pred(p, d):
            o = facet_peer(p)
            pred_copy(o, o, k).wait()
            return d

        lax.fori_loop(1, n_facet, wait_pred, 0)
        res_re = -vre[pl.ds(r0, run), :]
        res_im = -vim[pl.ds(r0, run), :]
        for p in range(1, n_facet):
            other = pred_all[facet_peer(p), k].astype(F32)
            res_re = res_re - other[:, :channels]
            res_im = res_im - other[:, channels:]
        for g in range(n_facet):
            share = (reader_ref[0, k] == g).astype(F32)
            seen = arrived[g].astype(F32) * share
            res_re = res_re + seen[:, :channels]
            res_im = res_im + seen[:, channels:]

        @pl.when(k == me_f)
        def _():
            resid_ref[0, :, :channels] = res_re
            resid_ref[0, :, channels:] = res_im

        h_re, h_im = hre[pl.ds(r0, run), :], him[pl.ds(r0, run), :]
        vre[pl.ds(r0, run), :] = res_re * h_re - res_im * h_im
        vim[pl.ds(r0, run), :] = res_re * h_im + res_im * h_re

        def pair(i, d):
            regrid(k * run + 2 * i)
            regrid(k * run + 2 * i + 1)
            return d

        lax.fori_loop(0, run // 2, pair, 0)
        return c

    lax.fori_loop(0, n_facet, grid_block, 0)

    ur, uc = iota((512, 128), 0), iota((512, 128), 1)
    unfold = jnp.where(ur // 128 == uc // 32, fold_values(uc % 32, ur % 128).astype(F32), 0.0).astype(BF16)
    spread = {}
    for j in range(16):
        c_re, s_re, c_im, s_im = (mats[(q * 16 + j) * R:(q * 16 + j + 1) * R, :] for q in range(4))
        for x, sign in ((16 + j, 1.0), (15 - j, -1.0)):
            m = c_re + sign * s_im
            n = c_im - sign * s_re
            spread[x] = jnp.concatenate([jnp.where(low, m, n), jnp.where(low, n, -m)], axis=0).astype(BF16)
    out_re, out_im = [], []
    for g in range(8):
        cells = jnp.dot(jnp.concatenate([spread[4 * g + i] for i in range(4)], axis=1), unfold,
                        preferred_element_type=F32)
        g_re, g_im = cells[:R], cells[R:]
        s_re, s_im = sre[:, 128 * g:128 * g + 128], sim[:, 128 * g:128 * g + 128]
        out_re.append(((s_re * g_re + s_im * g_im) * grid_scale).astype(BF16))
        out_im.append(((s_re * g_im - s_im * g_re) * grid_scale).astype(BF16))
    both = out_re + out_im
    stacked = jnp.concatenate(
        [jnp.concatenate(both[4 * q:4 * q + 4], axis=1) for q in range(4)], axis=0)
    own_r = iota((total, 4 * R), 0)
    place = (index_row_ref[...] == (own_r // chunk) * owned + own_r % owned) & (
        (own_r // owned) % 4 == iota((total, 4 * R), 1) // R)
    sums = jnp.dot(place.astype(F32).astype(BF16), stacked, preferred_element_type=F32)
    part_send[...] = sums.astype(BF16).reshape(n_tile, chunk, quarter)

    def send_part(p, c):
        part_copy(tile_peer(p), me_t).start()
        return c

    lax.fori_loop(1, n_tile, send_part, 0)

    def add_part(p, acc):
        o = tile_peer(p)
        part_copy(o, o).wait()
        return acc + part_all[o].astype(F32)

    acc = lax.fori_loop(1, n_tile, add_part, part_send[me_t].astype(F32))
    for q in range(4):
        dirty_ref[0, :, q * quarter:(q + 1) * quarter] = acc[q * owned:(q + 1) * owned]


def local(
    sectioned_rows,
    reader,
    baseline_coords,
    subgrid_index,
    stations,
    plane_index,
    model_grid,
    beam_screens,
    plane_phase,
    channel_freq,
):
    n_facet = lax.axis_size("facet")
    n_tile = lax.axis_size("tile")
    channels = channel_freq.shape[0]
    pixels = plane_phase.shape[1]
    run = sectioned_rows.shape[1]
    owned = model_grid.shape[1]
    R = n_facet * run
    chunk, quarter = 4 * owned, 2 * pixels // 4
    grid_scale = 1.0 / math.sqrt(channels * n_facet * (run * n_tile) / (owned * n_tile))

    cols = jnp.stack([baseline_coords[:, 0].reshape(R), baseline_coords[:, 1].reshape(R)], axis=1)
    index = jnp.stack(
        [stations[:, 0].reshape(R), stations[:, 1].reshape(R), plane_index.reshape(R)], axis=1)
    flat = jnp.tile(subgrid_index.reshape(R), 4)

    vmem = pl.BlockSpec(memory_space=pltpu.VMEM)
    body = functools.partial(kernel, n_facet, n_tile, owned, run, channels, grid_scale)
    dma = pltpu.SemaphoreType.DMA
    resid, dirty = pl.pallas_call(
        body,
        out_shape=(
            jax.ShapeDtypeStruct((1, run, 2 * channels), F32),
            jax.ShapeDtypeStruct((1, owned, 2 * pixels), F32),
        ),
        in_specs=[pl.BlockSpec(memory_space=pltpu.SMEM)] + [vmem] * 6
        + [pl.BlockSpec(memory_space=pl.ANY)] + [vmem] * 2,
        out_specs=(vmem, vmem),
        scratch_shapes=[
            pltpu.VMEM(beam_screens.shape[1:], BF16),
            pltpu.VMEM((chunk, quarter), BF16),
            pltpu.VMEM((n_tile, chunk, quarter), BF16),
            pltpu.VMEM((n_facet, run, 2 * channels), BF16),
            pltpu.VMEM((n_facet, run, 2 * channels), BF16),
            pltpu.VMEM((n_facet, n_facet, run, 2 * channels), BF16),
            pltpu.VMEM((n_tile, chunk, quarter), BF16),
            pltpu.VMEM((n_tile, chunk, quarter), BF16),
            pltpu.VMEM((channels // 128, R * 32, 128), F32),
            pltpu.VMEM((channels // 128, R * 32, 128), F32),
            pltpu.VMEM((64 * R, 128), F32),
            pltpu.VMEM((R, channels), F32),
            pltpu.VMEM((R, channels), F32),
            pltpu.VMEM((R, channels), F32),
            pltpu.VMEM((R, channels), F32),
            pltpu.VMEM((R, pixels), F32),
            pltpu.VMEM((R, pixels), F32),
            dma,
            dma((n_tile,)), dma((n_tile,)),
            dma((n_facet,)), dma((n_facet,)),
            dma((n_facet, n_facet)), dma((n_facet, n_facet)),
            dma((n_tile,)), dma((n_tile,)),
        ],
        compiler_params=pltpu.CompilerParams(
            collective_id=0, has_side_effects=True, vmem_limit_bytes=60 * 1024 * 1024),
        name="predict_regrid",
    )(reader, cols, index, flat[:, None], flat[None, :], sectioned_rows, model_grid,
      beam_screens[0], plane_phase, channel_freq[None, :])
    return (resid, dirty)


def solution(mesh):
    return jax.shard_map(
        local,
        mesh=mesh,
        in_specs=(
            P("facet", "tile", None),
            P("tile", None),
            P(None, None, "tile"),
            P(None, "tile"),
            P(None, None, "tile"),
            P(None, "tile"),
            P("facet", "tile", None),
            P("facet", None, None),
            P(),
            P(),
        ),
        out_specs=(P("facet", "tile", None), P("facet", "tile", None)),
        check_vma=False,
    )
```

time: 252 us -> 44.2 us (0.18)
  waiting for transfers between devices: 103 us -> 0 us
  other arithmetic: 61.5 us -> 0.02 us
  Pallas kernels: 0 us -> 33.9 us
  blocking collectives: 30.3 us -> 0 us
  local copies, waits for them, and re-layouts: 23.8 us -> 9.07 us
  between operations: 14.9 us -> 0.65 us
  matrix products: 14 us -> 0 us
  loops' own time: 4 us -> 0 us
    unnamed x3 -> x0, waiting for transfers between devices: 88.3 us -> none
    pallas_call x0 -> x1, Pallas kernels: none -> 33.9 us  [local(): pl.pallas_call(body, out_shape=(jax.ShapeDtypeStruct((1, run, 2 * channel...]
    all_gather x2 -> x0, blocking collectives: 30.3 us -> none  [the longest x1 24.6 us: local(): model_all = lax.all_gather(model_grid, 'tile', axis=1, tiled=True)[0]]
    dynamic_update_slice x12 -> x0, other arithmetic: 20.5 us -> none  [the longest x8 20.5 us: local(): tables = lax.map(geometry, block_ids)]
    convert_element_type x8 -> x0, other arithmetic: 17.5 us -> none  [the longest x2 17.4 us: phasor_tables(): jnp.sin(angles).astype(jnp.bfloat16)]
    neg x2 -> x0, other arithmetic: 14.4 us -> none  [north_matrix(): lower_half = jnp.concatenate([-north_sin, north_cos], axis=2)]
    psum x1 -> x0, waiting for transfers between devices: 14.2 us -> none  [local(): total = lax.psum(predicted, 'facet')]
    dot_general x5 -> x0, matrix products: 14 us -> none  [the longest x2 6.82 us: grid_rows(): jnp.einsum('rxc,ryc->rxy', operand, north_mat, preferred_element_type=jnp...]
  transfers between devices with their start and end apart: 2 -> 0, of which waited for: 2 -> 0; matrix products, arithmetic and copies ran while one was open for 1% -> 0% of each run, Pallas kernels for 0% -> 0%
where the time goes in v1:
time: 44.2 us; the launch traced here: 43.6 us
  Pallas kernels  33.9 us (77%)
  local copies, waits for them, and re-layouts  9.07 us (21%)
  between operations  0.65 us (1%)
    pallas_call x1, Pallas kernels, local(): pl.pallas_call(body, out_shape=(jax.ShapeDtypeStruct((1, run, 2 * channel...  33.9 us
    unnamed x2, local copies, waits for them, and re-layouts  2.94 us
    another operation x4, local copies, waits for them, and re-layouts, local(): jnp.stack([stations[:, 0].reshape(R), stations[:, 1].reshape(R), plane_in...  1.61 us

profile of v1, /device:TPU:0, one launch (start us, length us, event | category | flops | bytes accessed | tf_op | source)
XLA Modules:
  0.0 43.6 jit_solution(12631340356956771835)
XLA Ops:
  0.6 0.8 %tile.7 = s32[32]{0:T(128)S(1)} reshape(s32[2,16]{1,0:T(2,128)} %param.13) | data formatting | bytes 256 | tf_op jit(solution)/shard_map/tile | solution.py:362
  1.4 0.8 %stack_reshape.3 = s32[32,1]{0,1:T(1,128)S(1)} reshape(s32[2,16]{1,0:T(2,128)} %param.15) | data formatting | bytes 256 | tf_op jit(solution)/shard_map/stack;reshape | solution.py:360
  2.2 0.6 %broadcast_in_dim_tile.7.index_row_ref = s32[1,128]{1,0:T(1,128)} reshape(s32[4,32]{1,0:T(4,128)S(1)} %tile.8) | data formatting | bytes 1024 | tf_op jit(solution)/shard_map/broadcast_in_dim;tile | solution.py:403
  2.8 0.8 %slice_reduce_fusion.3 = (f32[2,16]{1,0:T(2,128)S(1)}, f32[2,16]{1,0:T(2,128)S(1)}) fusion(f32[2,2,16]{2,1,0:T(2,128)} %param.12), kind=kLoop, calls=%fused_computation.5 | loop fusion | bytes 512 | tf_op jit(solution)/shard_map/slice | solution.py:359
  3.5 0.1 stack_reshape_squeeze.12
  3.6 0.1 stack_reshape_squeeze.13
  3.7 0.8 %slice_reduce_fusion.1 = (s32[2,16]{1,0:T(2,128)S(1)}, s32[2,16]{1,0:T(2,128)S(1)}) fusion(s32[2,2,16]{2,1,0:T(2,128)} %param.14), kind=kLoop, calls=%fused_computation.3 | loop fusion | bytes 512 | tf_op jit(solution)/shard_map/slice | solution.py:361
  4.5 0.1 stack_reshape_squeeze.14
  4.6 0.1 stack_reshape_squeeze.15
  4.7 0.7 %copy.25.index_ref = s32[32,3]{1,0:T(8,128)} copy(s32[32,3]{0,1:T(4,128)S(1)} %pad_add_fusion) | data formatting | bytes 768 | tf_op jit(solution)/shard_map/stack | solution.py:360
  5.4 0.7 %copy.24.cols_ref = f32[32,2]{1,0:T(8,128)} copy(f32[32,2]{0,1:T(2,128)S(1)} %pad_maximum_fusion) | data formatting | bytes 512 | tf_op jit(solution)/shard_map/stack | solution.py:359
  6.1 0.7 %broadcast_in_dim_tile.8.index_col_ref = s32[128,1]{1,0:T(8,128)} reshape(s32[4,32]{1,0:T(4,128)S(1)} %tile.8) | data formatting | bytes 1024 | tf_op jit(solution)/shard_map/broadcast_in_dim;tile | solution.py:403
  6.8 33.9 %predict_regrid.1 = (f32[1,16,2048]{2,1,0:T(8,128)}, f32[1,4,2048]{2,1,0:T(4,128)}) custom-call(s32[1,2]{1,0:T(1,128)} %reader_ref.1, f32[32,2]{1,0:T(8,128)} %copy.24.cols_ref, s32[32,3]{1,0:T(8,128)} %copy.25.index_ref, s32[128,1]{1,0:T(8,128)} %broadcast_in_dim_tile.8.index_col_ref, s32[1,128]{1,0:T(1,128)} %broadcast_in_dim_tile.7.index_row_ref, ...), custom_call_target="tpu_custom_call" | custom-call | tf_op jit(solution)/shard_map/predict_regrid/pallas_call | solution.py:367
  40.7 1.6 %copy.29 = f32[1,16,2048]{2,1,0:T(8,128)} copy(f32[1,16,2048]{2,1,0:T(8,128)} %get-tuple-element.8) | data formatting | bytes 262144
  42.3 1.4 %copy.30 = f32[1,4,2048]{2,1,0:T(4,128)} copy(f32[1,4,2048]{2,1,0:T(4,128)} %get-tuple-element.9) | data formatting | bytes 65536
  (3 shorter events, 0.0 us)

commit v2 on v1

--- a/solution.py
+++ b/solution.py
@@ -37,12 +37,18 @@
     return jnp.where(part_col < 32, value, 0.0).astype(BF16)
 
 
+def column(rows):
+    n = rows[0].shape[1]
+    diagonal = iota((n, n), 0) == iota((n, n), 1)
+    return jnp.concatenate(
+        [jnp.sum(jnp.where(diagonal, row.astype(F32), 0.0), axis=1, keepdims=True) for row in rows], axis=0)
+
+
 def kernel(
     n_facet, n_tile, owned, run, channels, grid_scale,
-    reader_ref, cols_ref, index_ref, index_col_ref, index_row_ref,
-    rows_ref, model_ref, screens_hbm, phase_ref, freq_ref,
+    reader_ref, coords_ref, subgrid_ref, stations_ref, plane_ref, rows_ref, model_ref, screens_hbm, phase_ref, freq_ref,
     resid_ref, dirty_ref,
-    screens, model_send, model_all, arrived, pred_send, pred_all, part_send, part_all,
+    cols, screens, model_send, model_all, arrived, pred_send, pred_all, part_send, part_all,
     te, tn, mats, hre, him, vre, vim, sre, sim,
     local_sem, model_ss, model_rs, vis_ss, vis_rs, pred_ss, pred_rs, part_ss, part_rs,
 ):
@@ -78,50 +84,14 @@
     model_send[...] = jnp.concatenate(
         [model_f[:, q * quarter:(q + 1) * quarter] for q in range(4)], axis=0
     ).astype(BF16)
-    pl.semaphore_wait(barrier, n_tile + n_facet - 2)
-
-    def model_copy(o, slot):
-        return pltpu.make_async_remote_copy(
-            src_ref=model_send, dst_ref=model_all.at[slot], send_sem=model_ss.at[o],
-            recv_sem=model_rs.at[slot], device_id=(me_f, o), device_id_type=MESH)
-
-    def vis_copy(o, slot):
-        return pltpu.make_async_remote_copy(
-            src_ref=rows_ref.at[0], dst_ref=arrived.at[slot], send_sem=vis_ss.at[o],
-            recv_sem=vis_rs.at[slot], device_id=(o, me_t), device_id_type=MESH)
-
-    def pred_copy(o, slot, k):
-        return pltpu.make_async_remote_copy(
-            src_ref=pred_send.at[k], dst_ref=pred_all.at[slot, k], send_sem=pred_ss.at[o, k],
-            recv_sem=pred_rs.at[slot, k], device_id=(o, me_t), device_id_type=MESH)
-
-    def part_copy(o, slot):
-        return pltpu.make_async_remote_copy(
-            src_ref=part_send.at[o], dst_ref=part_all.at[slot], send_sem=part_ss.at[o],
-            recv_sem=part_rs.at[slot], device_id=(me_f, o), device_id_type=MESH)
-
-    def send_model(p, c):
-        model_copy(tile_peer(p), me_t).start()
-        return c
-
-    def send_vis(p, c):
-        vis_copy(facet_peer(p), me_f).start()
-        return c
-
-    lax.fori_loop(1, n_tile, send_model, 0)
-    lax.fori_loop(1, n_facet, send_vis, 0)
-    model_all[me_t] = model_send[...]
-    arrived[me_f] = rows_ref[0]
-
-    def tables(g, c):
-        r0 = pl.multiple_of(g * 8, 8)
-        freq = freq_ref[...]
-        halves = []
-        for col, dst in ((0, te), (1, tn)):
-            u = cols_ref[pl.ds(r0, 8), col:col + 1]
-            alpha = (u * (2.0 * math.pi / 64.0)) * freq
+    for axis in range(2):
+        cols[:, axis:axis + 1] = column([coords_ref[k, axis:axis + 1, :] for k in range(n_facet)])
+
+    def tables(axis, dst):
+        def group(g, c):
+            r0 = pl.multiple_of(g * 8, 8)
+            alpha = (cols[pl.ds(r0, 8), axis:axis + 1] * (2.0 * math.pi / 64.0)) * freq_ref[...]
             c0, s0 = cos_sin(alpha)
-            halves.append((c0, s0))
             twice = 2.0 - 4.0 * s0 * s0
             c_old, s_old, c_now, s_now = c0, -s0, c0, s0
             for j in range(16):
@@ -132,25 +102,67 @@
                 if j < 15:
                     c_old, c_now = c_now, twice * c_now - c_old
                     s_old, s_now = s_now, twice * s_now - s_old
-        (ca, sa), (cb, sb) = halves
-        hre[pl.ds(r0, 8), :] = ca * cb - sa * sb
-        him[pl.ds(r0, 8), :] = ca * sb + sa * cb
-        return c
-
-    lax.fori_loop(0, R // 8, tables, 0)
+            if axis == 0:
+                hre[pl.ds(r0, 8), :] = c0
+                him[pl.ds(r0, 8), :] = s0
+            else:
+                ca, sa = hre[pl.ds(r0, 8), :], him[pl.ds(r0, 8), :]
+                hre[pl.ds(r0, 8), :] = ca * c0 - sa * s0
+                him[pl.ds(r0, 8), :] = ca * s0 + sa * c0
+            return c
+
+        lax.fori_loop(0, R // 8, group, 0)
+
+    tables(0, te)
+    pl.semaphore_wait(barrier, n_tile + n_facet - 2)
+
+    def model_copy(o, slot):
+        return pltpu.make_async_remote_copy(
+            src_ref=model_send, dst_ref=model_all.at[slot], send_sem=model_ss.at[o],
+            recv_sem=model_rs.at[slot], device_id=(me_f, o), device_id_type=MESH)
+
+    def vis_copy(o, slot):
+        return pltpu.make_async_remote_copy(
+            src_ref=rows_ref.at[0], dst_ref=arrived.at[slot], send_sem=vis_ss.at[o],
+            recv_sem=vis_rs.at[slot], device_id=(o, me_t), device_id_type=MESH)
+
+    def pred_copy(o, slot, k):
+        return pltpu.make_async_remote_copy(
+            src_ref=pred_send.at[k], dst_ref=pred_all.at[slot, k], send_sem=pred_ss.at[o, k],
+            recv_sem=pred_rs.at[slot, k], device_id=(o, me_t), device_id_type=MESH)
+
+    def part_copy(o, slot):
+        return pltpu.make_async_remote_copy(
+            src_ref=part_send.at[o], dst_ref=part_all.at[slot], send_sem=part_ss.at[o],
+            recv_sem=part_rs.at[slot], device_id=(me_f, o), device_id_type=MESH)
+
+    def send_model(p, c):
+        model_copy(tile_peer(p), me_t).start()
+        return c
+
+    def send_vis(p, c):
+        vis_copy(facet_peer(p), me_f).start()
+        return c
+
+    lax.fori_loop(1, n_tile, send_model, 0)
+    lax.fori_loop(1, n_facet, send_vis, 0)
+    model_all[me_t] = model_send[...]
+    arrived[me_f] = rows_ref[0]
+
+    tables(1, tn)
 
     stations = screens.shape[0]
     planes, pixels = phase_ref.shape
     half_c, half_s = cos_sin(phase_ref[...] * 0.5)
     waves = jnp.concatenate([1.0 - 2.0 * half_s * half_s, 2.0 * half_s * half_c], axis=1)
-    plane_hot = (index_ref[:, 2:3] == iota((R, planes), 1)).astype(F32)
+    plane_hot = (column([plane_ref[k:k + 1, :] for k in range(n_facet)]) == iota((R, planes), 1).astype(F32)).astype(F32)
     wave = jnp.dot(plane_hot, waves, preferred_element_type=F32, precision=lax.Precision.HIGHEST)
     wave_re, wave_im = wave[:, :pixels], wave[:, pixels:]
     load.wait()
-    one_hot = (index_ref[:, 0:1] == iota((R, stations), 1)).astype(F32).astype(BF16)
-    two_hot = (index_ref[:, 1:2] == iota((R, stations), 1)).astype(F32).astype(BF16)
-    one = jnp.dot(one_hot, screens[...], preferred_element_type=F32)
-    two = jnp.dot(two_hot, screens[...], preferred_element_type=F32)
+    pair_col = column([stations_ref[k, a:a + 1, :] for a in range(2) for k in range(n_facet)])
+    station_hot = (pair_col == iota((2 * R, stations), 1).astype(F32)).astype(F32).astype(BF16)
+    both_rows = jnp.dot(station_hot, screens[...], preferred_element_type=F32)
+    one, two = both_rows[:R], both_rows[R:]
     one_re, one_im, two_re, two_im = one[:, :pixels], one[:, pixels:], two[:, :pixels], two[:, pixels:]
     pair_re = one_re * two_re + one_im * two_im
     pair_im = one_im * two_re - one_re * two_im
@@ -165,7 +177,8 @@
     lax.fori_loop(1, n_tile, wait_model, 0)
     total = n_tile * chunk
     own_i = iota((4 * R, total), 1)
-    pick = (index_col_ref[...] == (own_i // chunk) * owned + own_i % owned) & (
+    sub_col = jnp.concatenate([column([subgrid_ref[k:k + 1, :] for k in range(n_facet)])] * 4, axis=0)
+    pick = (sub_col == ((own_i // chunk) * owned + own_i % owned).astype(F32)) & (
         (own_i // owned) % 4 == iota((4 * R, total), 0) // R)
     found = jnp.dot(pick.astype(F32).astype(BF16), model_all[...].reshape(total, quarter),
                     preferred_element_type=F32)
@@ -207,12 +220,12 @@
             vim[pl.ds(r, 1), lo:lo + step] = jnp.sum(east * inner[32:], axis=0, keepdims=True)
 
     def predict(k, c):
-        def pair(i, d):
-            degrid(k * run + 2 * i)
-            degrid(k * run + 2 * i + 1)
+        def group(i, d):
+            for n in range(4):
+                degrid(k * run + 4 * i + n)
             return d
 
-        lax.fori_loop(0, run // 2, pair, 0)
+        lax.fori_loop(0, run // 4, group, 0)
         r0 = pl.multiple_of(k * run, run)
         a_re, a_im = vre[pl.ds(r0, run), :], vim[pl.ds(r0, run), :]
         h_re, h_im = hre[pl.ds(r0, run), :], him[pl.ds(r0, run), :]
@@ -282,12 +295,12 @@
         vre[pl.ds(r0, run), :] = res_re * h_re - res_im * h_im
         vim[pl.ds(r0, run), :] = res_re * h_im + res_im * h_re
 
-        def pair(i, d):
-            regrid(k * run + 2 * i)
-            regrid(k * run + 2 * i + 1)
+        def group(i, d):
+            for n in range(4):
+                regrid(k * run + 4 * i + n)
             return d
 
-        lax.fori_loop(0, run // 2, pair, 0)
+        lax.fori_loop(0, run // 4, group, 0)
         return c
 
     lax.fori_loop(0, n_facet, grid_block, 0)
@@ -313,7 +326,9 @@
     stacked = jnp.concatenate(
         [jnp.concatenate(both[4 * q:4 * q + 4], axis=1) for q in range(4)], axis=0)
     own_r = iota((total, 4 * R), 0)
-    place = (index_row_ref[...] == (own_r // chunk) * owned + own_r % owned) & (
+    sub_row = jnp.sum(
+        jnp.where(iota((4 * R, 4 * R), 0) == iota((4 * R, 4 * R), 1), sub_col, 0.0), axis=0, keepdims=True)
+    place = (sub_row == ((own_r // chunk) * owned + own_r % owned).astype(F32)) & (
         (own_r // owned) % 4 == iota((total, 4 * R), 1) // R)
     sums = jnp.dot(place.astype(F32).astype(BF16), stacked, preferred_element_type=F32)
     part_send[...] = sums.astype(BF16).reshape(n_tile, chunk, quarter)
@@ -332,6 +347,15 @@
     acc = lax.fori_loop(1, n_tile, add_part, part_send[me_t].astype(F32))
     for q in range(4):
         dirty_ref[0, :, q * quarter:(q + 1) * quarter] = acc[q * owned:(q + 1) * owned]
+
+
+def hand_over(resid_in, dirty_in, resid_out, dirty_out, resid_sem, dirty_sem):
+    first = pltpu.make_async_copy(resid_in, resid_out, resid_sem)
+    second = pltpu.make_async_copy(dirty_in, dirty_out, dirty_sem)
+    first.start()
+    second.start()
+    first.wait()
+    second.wait()
 
 
 def local(
@@ -356,11 +380,6 @@
     chunk, quarter = 4 * owned, 2 * pixels // 4
     grid_scale = 1.0 / math.sqrt(channels * n_facet * (run * n_tile) / (owned * n_tile))
 
-    cols = jnp.stack([baseline_coords[:, 0].reshape(R), baseline_coords[:, 1].reshape(R)], axis=1)
-    index = jnp.stack(
-        [stations[:, 0].reshape(R), stations[:, 1].reshape(R), plane_index.reshape(R)], axis=1)
-    flat = jnp.tile(subgrid_index.reshape(R), 4)
-
     vmem = pl.BlockSpec(memory_space=pltpu.VMEM)
     body = functools.partial(kernel, n_facet, n_tile, owned, run, channels, grid_scale)
     dma = pltpu.SemaphoreType.DMA
@@ -374,6 +393,7 @@
         + [pl.BlockSpec(memory_space=pl.ANY)] + [vmem] * 2,
         out_specs=(vmem, vmem),
         scratch_shapes=[
+            pltpu.VMEM((R, 2), F32),
             pltpu.VMEM(beam_screens.shape[1:], BF16),
             pltpu.VMEM((chunk, quarter), BF16),
             pltpu.VMEM((n_tile, chunk, quarter), BF16),
@@ -400,9 +420,20 @@
         compiler_params=pltpu.CompilerParams(
             collective_id=0, has_side_effects=True, vmem_limit_bytes=60 * 1024 * 1024),
         name="predict_regrid",
-    )(reader, cols, index, flat[:, None], flat[None, :], sectioned_rows, model_grid,
+    )(reader, baseline_coords, subgrid_index, stations, plane_index, sectioned_rows, model_grid,
       beam_screens[0], plane_phase, channel_freq[None, :])
-    return (resid, dirty)
+    anywhere = pl.BlockSpec(memory_space=pl.ANY)
+    return pl.pallas_call(
+        hand_over,
+        out_shape=(
+            jax.ShapeDtypeStruct(resid.shape, F32),
+            jax.ShapeDtypeStruct(dirty.shape, F32),
+        ),
+        in_specs=[anywhere] * 2,
+        out_specs=(anywhere, anywhere),
+        scratch_shapes=[dma, dma],
+        name="hand_over",
+    )(resid, dirty)
 
 
 def solution(mesh):

time: 44.2 us -> 39 us (0.88)
  local copies, waits for them, and re-layouts: 9.07 us -> 0 us
  Pallas kernels: 33.9 us -> 38.1 us
    pallas_call x0 -> x1, Pallas kernels: none -> 6.08 us  [local(): pl.pallas_call(hand_over, out_shape=(jax.ShapeDtypeStruct(resid.shape, F3...]
    another operation x11 -> x0, local copies, waits for them, and re-layouts: 4.58 us -> none  [the longest x4 1.61 us: local(): jnp.stack([stations[:, 0].reshape(R), stations[:, 1].reshape(R), plane_in...]
    unnamed x2 -> x0, local copies, waits for them, and re-layouts: 2.94 us -> none
    pallas_call x1, Pallas kernels: 33.9 us -> 32 us  [local(): pl.pallas_call(body, out_shape=(jax.ShapeDtypeStruct((1, run, 2 * channel...]
    slice x2 -> x0, local copies, waits for them, and re-layouts: 1.55 us -> none  [the longest x1 0.77 us: local(): baseline_coords[:, 0].reshape(R)]
where the time goes in v2:
time: 39 us; the launch traced here: 38.8 us
  Pallas kernels  38.1 us (98%)
  between operations  0.64 us (2%)
    pallas_call x1, Pallas kernels, local(): pl.pallas_call(body, out_shape=(jax.ShapeDtypeStruct((1, run, 2 * channel...  32 us
    pallas_call x1, Pallas kernels, local(): pl.pallas_call(hand_over, out_shape=(jax.ShapeDtypeStruct(resid.shape, F3...  6.08 us

profile of v2, /device:TPU:0, one launch (start us, length us, event | category | flops | bytes accessed | tf_op | source)
XLA Modules:
  0.0 38.8 jit_solution(5764850113365807421)
XLA Ops:
  0.6 32.0 %predict_regrid.1 = (f32[1,16,2048]{2,1,0:T(8,128)}, f32[1,4,2048]{2,1,0:T(4,128)}) custom-call(s32[1,2]{1,0:T(1,128)} %reader_ref.1, f32[2,2,16]{2,1,0:T(2,128)} %coords_ref.1, s32[2,16]{1,0:T(2,128)} %subgrid_ref.1, s32[2,2,16]{2,1,0:T(2,128)} %stations_ref.1, s32[2,16]{1,0:T(2,128)} %plane_ref.1, bf16[1,16,2048]{2,1,0:T(8,128)(2,1)} %rows_ref.1, ...), custom_call_target="tpu_custom_call" | custom-call | tf_op jit(solution)/shard_map/predict_regrid/pallas_call | solution.py:386
  32.7 6.1 %hand_over.1 = (f32[1,16,2048]{2,1,0:T(8,128)}, f32[1,4,2048]{2,1,0:T(4,128)}) custom-call(f32[1,16,2048]{2,1,0:T(8,128)} %get-tuple-element.4.resid_in, f32[1,4,2048]{2,1,0:T(4,128)} %get-tuple-element.5.dirty_in), custom_call_target="tpu_custom_call" | custom-call | tf_op jit(solution)/shard_map/hand_over/pallas_call | solution.py:426

commit v3 on v2

--- a/solution.py
+++ b/solution.py
@@ -87,28 +87,34 @@
     for axis in range(2):
         cols[:, axis:axis + 1] = column([coords_ref[k, axis:axis + 1, :] for k in range(n_facet)])
 
+    pr, pc = iota((256, 256), 0), iota((256, 256), 1)
+    perm = ((pr // 32 == pc % 8) & (pr % 32 == pc // 8)).astype(F32).astype(BF16)
+    perm_back = ((pr // 8 == pc % 32) & (pr % 8 == pc // 32)).astype(F32).astype(BF16)
+    step = 256
+
     def tables(axis, dst):
         def group(g, c):
             r0 = pl.multiple_of(g * 8, 8)
-            alpha = (cols[pl.ds(r0, 8), axis:axis + 1] * (2.0 * math.pi / 64.0)) * freq_ref[...]
-            c0, s0 = cos_sin(alpha)
-            twice = 2.0 - 4.0 * s0 * s0
-            c_old, s_old, c_now, s_now = c0, -s0, c0, s0
-            for j in range(16):
-                for b in range(channels // 128):
-                    lanes = slice(128 * b, 128 * b + 128)
-                    dst[b, pl.ds(r0 * 32 + j, 8, stride=32), :] = c_now[:, lanes]
-                    dst[b, pl.ds(r0 * 32 + 16 + j, 8, stride=32), :] = s_now[:, lanes]
-                if j < 15:
-                    c_old, c_now = c_now, twice * c_now - c_old
-                    s_old, s_now = s_now, twice * s_now - s_old
-            if axis == 0:
-                hre[pl.ds(r0, 8), :] = c0
-                him[pl.ds(r0, 8), :] = s0
-            else:
-                ca, sa = hre[pl.ds(r0, 8), :], him[pl.ds(r0, 8), :]
-                hre[pl.ds(r0, 8), :] = ca * c0 - sa * s0
-                him[pl.ds(r0, 8), :] = ca * s0 + sa * c0
+            at = pl.multiple_of(g * 256, 256)
+            u = cols[pl.ds(r0, 8), axis:axis + 1] * (2.0 * math.pi / 64.0)
+            for lo in range(0, channels, step):
+                lanes = slice(lo, lo + step)
+                c0, s0 = cos_sin(u * freq_ref[:, lanes])
+                twice = 2.0 - 4.0 * s0 * s0
+                cos_rows, sin_rows = [c0, twice * c0 - c0], [s0, twice * s0 + s0]
+                for j in range(2, 16):
+                    cos_rows.append(twice * cos_rows[-1] - cos_rows[-2])
+                    sin_rows.append(twice * sin_rows[-1] - sin_rows[-2])
+                rows = jnp.concatenate(cos_rows + sin_rows, axis=0).astype(BF16)
+                moved = jnp.dot(perm, rows, preferred_element_type=F32)
+                dst[pl.ds(at, 256), lanes] = moved.astype(dst.dtype)
+                if axis == 0:
+                    hre[pl.ds(r0, 8), lanes] = c0
+                    him[pl.ds(r0, 8), lanes] = s0
+                else:
+                    ca, sa = hre[pl.ds(r0, 8), lanes], him[pl.ds(r0, 8), lanes]
+                    hre[pl.ds(r0, 8), lanes] = ca * c0 - sa * s0
+                    him[pl.ds(r0, 8), lanes] = ca * s0 + sa * c0
             return c
 
         lax.fori_loop(0, R // 8, group, 0)
@@ -191,7 +197,7 @@
     fr, fc = iota((128, 512), 0), iota((128, 512), 1)
     fold = jnp.where(fr // 32 == fc // 128, fold_values(fr % 32, fc % 128).astype(F32), 0.0).astype(BF16)
     low = iota((R, 128), 1) < 16
-    by_x = {}
+    by_x, folded = {}, {}
     for g in range(8):
         got = jnp.dot(image[:, 128 * g:128 * g + 128], fold, preferred_element_type=F32)
         for i in range(4):
@@ -203,19 +209,19 @@
         parts = (jnp.where(low, e_re, -e_im), -jnp.where(low, o_im, o_re),
                  jnp.where(low, e_im, e_re), jnp.where(low, o_re, -o_im))
         for q in range(4):
-            mats[(q * 16 + j) * R:(q * 16 + j + 1) * R, :] = parts[q]
-
-    step = 256
-
-    def table(ref, at, lo):
-        return jnp.concatenate([ref[lo // 128 + b, pl.ds(at, 32), :] for b in range(step // 128)], axis=1)
+            folded[q * 16 + j] = parts[q].astype(BF16)
+    for lot in range(8):
+        for r0 in range(0, R, 32):
+            cells = jnp.concatenate([folded[8 * lot + m][r0:r0 + 32] for m in range(8)], axis=0)
+            moved = jnp.dot(perm_back, cells, preferred_element_type=F32)
+            mats[r0:r0 + 32, 8 * lot:8 * lot + 8, :] = moved.reshape(32, 8, 128)
 
     def degrid(r):
-        lhs = mats[pl.ds(r, 64, stride=R), :][:, :32].astype(BF16)
+        lhs = mats[r][:, :32].astype(BF16)
         at = pl.multiple_of(r * 32, 32)
         for lo in range(0, channels, step):
-            inner = jnp.dot(lhs, table(tn, at, lo).astype(BF16), preferred_element_type=F32)
-            east = table(te, at, lo)
+            inner = jnp.dot(lhs, tn[pl.ds(at, 32), lo:lo + step], preferred_element_type=F32)
+            east = te[pl.ds(at, 32), lo:lo + step]
             vre[pl.ds(r, 1), lo:lo + step] = jnp.sum(east * inner[:32], axis=0, keepdims=True)
             vim[pl.ds(r, 1), lo:lo + step] = jnp.sum(east * inner[32:], axis=0, keepdims=True)
 
@@ -256,14 +262,20 @@
         at = pl.multiple_of(r * 32, 32)
         acc = jnp.zeros((64, 32), F32)
         for lo in range(0, channels, step):
-            east = table(te, at, lo)
+            east = te[pl.ds(at, 32), lo:lo + step]
             weighted = jnp.concatenate(
                 [east * vre[pl.ds(r, 1), lo:lo + step], east * vim[pl.ds(r, 1), lo:lo + step]], axis=0
             ).astype(BF16)
             acc = acc + lax.dot_general(
-                weighted, table(tn, at, lo).astype(BF16),
+                weighted, tn[pl.ds(at, 32), lo:lo + step],
                 (((1,), (1,)), ((), ())), preferred_element_type=F32)
-        mats[pl.ds(r, 64, stride=R), :] = jnp.concatenate([acc, jnp.zeros((64, 96), F32)], axis=1)
+        cos_lane = iota((16, 32), 1) < 16
+        c_re, s_re, c_im, s_im = (acc[16 * q:16 * q + 16] for q in range(4))
+        m_up, m_down, n_up, n_down = c_re + s_im, c_re - s_im, c_im - s_re, c_im + s_re
+        cells = jnp.concatenate(
+            [jnp.where(cos_lane, m_up, n_up), jnp.where(cos_lane, m_down, n_down),
+             jnp.where(cos_lane, n_up, -m_up), jnp.where(cos_lane, n_down, -m_down)], axis=0)
+        mats[r] = jnp.concatenate([cells, jnp.zeros((64, 96), F32)], axis=1)
 
     def grid_block(k, c):
         r0 = pl.multiple_of(k * run, run)
@@ -308,12 +320,14 @@
     ur, uc = iota((512, 128), 0), iota((512, 128), 1)
     unfold = jnp.where(ur // 128 == uc // 32, fold_values(uc % 32, ur % 128).astype(F32), 0.0).astype(BF16)
     spread = {}
-    for j in range(16):
-        c_re, s_re, c_im, s_im = (mats[(q * 16 + j) * R:(q * 16 + j + 1) * R, :] for q in range(4))
-        for x, sign in ((16 + j, 1.0), (15 - j, -1.0)):
-            m = c_re + sign * s_im
-            n = c_im - sign * s_re
-            spread[x] = jnp.concatenate([jnp.where(low, m, n), jnp.where(low, n, -m)], axis=0).astype(BF16)
+    for lot in range(8):
+        moved = [jnp.dot(perm, mats[r0:r0 + 32, 8 * lot:8 * lot + 8, :].reshape(256, 128).astype(BF16),
+                         preferred_element_type=F32).astype(BF16) for r0 in range(0, R, 32)]
+        for m in range(8):
+            part, place_x = divmod(8 * lot + m, 32)
+            x = 16 + place_x if place_x < 16 else 31 - place_x
+            spread[part, x] = [got[32 * m:32 * m + 32] for got in moved]
+    spread = {x: jnp.concatenate(spread[0, x] + spread[1, x], axis=0) for x in range(32)}
     out_re, out_im = [], []
     for g in range(8):
         cells = jnp.dot(jnp.concatenate([spread[4 * g + i] for i in range(4)], axis=1), unfold,
@@ -349,13 +363,9 @@
         dirty_ref[0, :, q * quarter:(q + 1) * quarter] = acc[q * owned:(q + 1) * owned]
 
 
-def hand_over(resid_in, dirty_in, resid_out, dirty_out, resid_sem, dirty_sem):
-    first = pltpu.make_async_copy(resid_in, resid_out, resid_sem)
-    second = pltpu.make_async_copy(dirty_in, dirty_out, dirty_sem)
-    first.start()
-    second.start()
-    first.wait()
-    second.wait()
+def hand_over(resid_in, dirty_in, resid_out, dirty_out):
+    resid_out[...] = resid_in[...]
+    dirty_out[...] = dirty_in[...]
 
 
 def local(
@@ -402,9 +412,9 @@
             pltpu.VMEM((n_facet, n_facet, run, 2 * channels), BF16),
             pltpu.VMEM((n_tile, chunk, quarter), BF16),
             pltpu.VMEM((n_tile, chunk, quarter), BF16),
-            pltpu.VMEM((channels // 128, R * 32, 128), F32),
-            pltpu.VMEM((channels // 128, R * 32, 128), F32),
-            pltpu.VMEM((64 * R, 128), F32),
+            pltpu.VMEM((R * 32, channels), F32),
+            pltpu.VMEM((R * 32, channels), BF16),
+            pltpu.VMEM((R, 64, 128), F32),
             pltpu.VMEM((R, channels), F32),
             pltpu.VMEM((R, channels), F32),
             pltpu.VMEM((R, channels), F32),
@@ -422,16 +432,14 @@
         name="predict_regrid",
     )(reader, baseline_coords, subgrid_index, stations, plane_index, sectioned_rows, model_grid,
       beam_screens[0], plane_phase, channel_freq[None, :])
-    anywhere = pl.BlockSpec(memory_space=pl.ANY)
     return pl.pallas_call(
         hand_over,
         out_shape=(
             jax.ShapeDtypeStruct(resid.shape, F32),
             jax.ShapeDtypeStruct(dirty.shape, F32),
         ),
-        in_specs=[anywhere] * 2,
-        out_specs=(anywhere, anywhere),
-        scratch_shapes=[dma, dma],
+        in_specs=[vmem] * 2,
+        out_specs=(vmem, vmem),
         name="hand_over",
     )(resid, dirty)
 

time: 39 us -> 33 us (0.85)
  Pallas kernels: 38.1 us -> 32.2 us
    pallas_call x1, Pallas kernels: 6.08 us -> 1.57 us  [local(): pl.pallas_call(hand_over, out_shape=(jax.ShapeDtypeStruct(resid.shape, F3...]
    pallas_call x1, Pallas kernels: 32 us -> 30.6 us  [local(): pl.pallas_call(body, out_shape=(jax.ShapeDtypeStruct((1, run, 2 * channel...]
where the time goes in v3:
time: 33 us; the launch traced here: 32.8 us
  Pallas kernels  32.2 us (98%)
  between operations  0.64 us (2%)
    pallas_call x1, Pallas kernels, local(): pl.pallas_call(body, out_shape=(jax.ShapeDtypeStruct((1, run, 2 * channel...  30.6 us
    pallas_call x1, Pallas kernels, local(): pl.pallas_call(hand_over, out_shape=(jax.ShapeDtypeStruct(resid.shape, F3...  1.57 us

profile of v3, /device:TPU:0, one launch (start us, length us, event | category | flops | bytes accessed | tf_op | source)
XLA Modules:
  0.0 32.8 jit_solution(7374845361917854194)
XLA Ops:
  0.6 30.6 %predict_regrid.1 = (f32[1,16,2048]{2,1,0:T(8,128)}, f32[1,4,2048]{2,1,0:T(4,128)}) custom-call(s32[1,2]{1,0:T(1,128)} %reader_ref.1, f32[2,2,16]{2,1,0:T(2,128)} %coords_ref.1, s32[2,16]{1,0:T(2,128)} %subgrid_ref.1, s32[2,2,16]{2,1,0:T(2,128)} %stations_ref.1, s32[2,16]{1,0:T(2,128)} %plane_ref.1, bf16[1,16,2048]{2,1,0:T(8,128)(2,1)} %rows_ref.1, ...), custom_call_target="tpu_custom_call" | custom-call | tf_op jit(solution)/shard_map/predict_regrid/pallas_call | solution.py:396
  31.3 1.6 %hand_over.1 = (f32[1,16,2048]{2,1,0:T(8,128)}, f32[1,4,2048]{2,1,0:T(4,128)}) custom-call(f32[1,16,2048]{2,1,0:T(8,128)} %get-tuple-element.4.resid_in, f32[1,4,2048]{2,1,0:T(4,128)} %get-tuple-element.5.dirty_in), custom_call_target="tpu_custom_call" | custom-call | tf_op jit(solution)/shard_map/hand_over/pallas_call | solution.py:435

commit v4 on v3

--- a/solution.py
+++ b/solution.py
@@ -49,7 +49,7 @@
     reader_ref, coords_ref, subgrid_ref, stations_ref, plane_ref, rows_ref, model_ref, screens_hbm, phase_ref, freq_ref,
     resid_ref, dirty_ref,
     cols, screens, model_send, model_all, arrived, pred_send, pred_all, part_send, part_all,
-    te, tn, mats, hre, him, vre, vim, sre, sim,
+    te, tn, mats, weighted, hre, him, vre, vim, sre, sim,
     local_sem, model_ss, model_rs, vis_ss, vis_rs, pred_ss, pred_rs, part_ss, part_rs,
 ):
     R = n_facet * run
@@ -194,14 +194,15 @@
         [sre[...] * model_re - sim[...] * model_im, sre[...] * model_im + sim[...] * model_re], axis=0
     ).astype(BF16)
 
-    fr, fc = iota((128, 512), 0), iota((128, 512), 1)
-    fold = jnp.where(fr // 32 == fc // 128, fold_values(fr % 32, fc % 128).astype(F32), 0.0).astype(BF16)
-    low = iota((R, 128), 1) < 16
+    fr, fc = iota((128, 1024), 0), iota((128, 1024), 1)
+    fold = jnp.where(fr // 32 == fc // 256, fold_values(fr % 32, fc % 32).astype(F32), 0.0).astype(BF16)
+    low = iota((R, 256), 1) % 32 < 16
+    diagonal = pr // 8 % 8 == pc // 32
     by_x, folded = {}, {}
     for g in range(8):
         got = jnp.dot(image[:, 128 * g:128 * g + 128], fold, preferred_element_type=F32)
         for i in range(4):
-            by_x[4 * g + i] = got[:, 128 * i:128 * i + 128]
+            by_x[4 * g + i] = got[:, 256 * i:256 * i + 256]
     for j in range(16):
         up, down = by_x[16 + j], by_x[15 - j]
         even, odd = up + down, up - down
@@ -214,24 +215,27 @@
         for r0 in range(0, R, 32):
             cells = jnp.concatenate([folded[8 * lot + m][r0:r0 + 32] for m in range(8)], axis=0)
             moved = jnp.dot(perm_back, cells, preferred_element_type=F32)
-            mats[r0:r0 + 32, 8 * lot:8 * lot + 8, :] = moved.reshape(32, 8, 128)
-
-    def degrid(r):
-        lhs = mats[r][:, :32].astype(BF16)
-        at = pl.multiple_of(r * 32, 32)
+            mats[r0:r0 + 32, 8 * lot:8 * lot + 8, :] = jnp.where(diagonal, moved, 0.0).reshape(32, 8, 256)
+
+    def degrid(g):
+        r0 = pl.multiple_of(g * 8, 8)
+        at = pl.multiple_of(g * 256, 256)
+        lhs = mats[pl.ds(r0, 8)].reshape(512, 256).astype(BF16)
         for lo in range(0, channels, step):
-            inner = jnp.dot(lhs, tn[pl.ds(at, 32), lo:lo + step], preferred_element_type=F32)
-            east = te[pl.ds(at, 32), lo:lo + step]
-            vre[pl.ds(r, 1), lo:lo + step] = jnp.sum(east * inner[:32], axis=0, keepdims=True)
-            vim[pl.ds(r, 1), lo:lo + step] = jnp.sum(east * inner[32:], axis=0, keepdims=True)
+            inner = jnp.dot(lhs, tn[pl.ds(at, 256), lo:lo + step], preferred_element_type=F32)
+            for n in range(8):
+                east = te[pl.ds(at + 32 * n, 32), lo:lo + step]
+                vre[pl.ds(r0 + n, 1), lo:lo + step] = jnp.sum(
+                    east * inner[64 * n:64 * n + 32], axis=0, keepdims=True)
+                vim[pl.ds(r0 + n, 1), lo:lo + step] = jnp.sum(
+                    east * inner[64 * n + 32:64 * n + 64], axis=0, keepdims=True)
 
     def predict(k, c):
         def group(i, d):
-            for n in range(4):
-                degrid(k * run + 4 * i + n)
+            degrid(k * (run // 8) + i)
             return d
 
-        lax.fori_loop(0, run // 4, group, 0)
+        lax.fori_loop(0, run // 8, group, 0)
         r0 = pl.multiple_of(k * run, run)
         a_re, a_im = vre[pl.ds(r0, run), :], vim[pl.ds(r0, run), :]
         h_re, h_im = hre[pl.ds(r0, run), :], him[pl.ds(r0, run), :]
@@ -258,24 +262,26 @@
 
     lax.fori_loop(1, n_facet, wait_vis, 0)
 
-    def regrid(r):
-        at = pl.multiple_of(r * 32, 32)
-        acc = jnp.zeros((64, 32), F32)
-        for lo in range(0, channels, step):
-            east = te[pl.ds(at, 32), lo:lo + step]
-            weighted = jnp.concatenate(
-                [east * vre[pl.ds(r, 1), lo:lo + step], east * vim[pl.ds(r, 1), lo:lo + step]], axis=0
-            ).astype(BF16)
-            acc = acc + lax.dot_general(
-                weighted, tn[pl.ds(at, 32), lo:lo + step],
-                (((1,), (1,)), ((), ())), preferred_element_type=F32)
-        cos_lane = iota((16, 32), 1) < 16
-        c_re, s_re, c_im, s_im = (acc[16 * q:16 * q + 16] for q in range(4))
-        m_up, m_down, n_up, n_down = c_re + s_im, c_re - s_im, c_im - s_re, c_im + s_re
-        cells = jnp.concatenate(
-            [jnp.where(cos_lane, m_up, n_up), jnp.where(cos_lane, m_down, n_down),
-             jnp.where(cos_lane, n_up, -m_up), jnp.where(cos_lane, n_down, -m_down)], axis=0)
-        mats[r] = jnp.concatenate([cells, jnp.zeros((64, 96), F32)], axis=1)
+    def regrid(g):
+        r0 = pl.multiple_of(g * 8, 8)
+        at = pl.multiple_of(g * 256, 256)
+        for n in range(8):
+            for lo in range(0, channels, step):
+                east = te[pl.ds(at + 32 * n, 32), lo:lo + step]
+                weighted[64 * n:64 * n + 32, lo:lo + step] = (east * vre[pl.ds(r0 + n, 1), lo:lo + step]).astype(BF16)
+                weighted[64 * n + 32:64 * n + 64, lo:lo + step] = (east * vim[pl.ds(r0 + n, 1), lo:lo + step]).astype(BF16)
+        acc = lax.dot_general(weighted[...], tn[pl.ds(at, 256), :], (((1,), (1,)), ((), ())),
+                              preferred_element_type=F32)
+        lane = iota((16, 256), 1)
+        cos_lane = lane % 32 < 16
+        for n in range(8):
+            own = lane // 32 == n
+            c_re, s_re, c_im, s_im = (
+                jnp.where(own, acc[64 * n + 16 * q:64 * n + 16 * q + 16], 0.0) for q in range(4))
+            m_up, m_down, n_up, n_down = c_re + s_im, c_re - s_im, c_im - s_re, c_im + s_re
+            mats[r0 + n] = jnp.concatenate(
+                [jnp.where(cos_lane, m_up, n_up), jnp.where(cos_lane, m_down, n_down),
+                 jnp.where(cos_lane, n_up, -m_up), jnp.where(cos_lane, n_down, -m_down)], axis=0)
 
     def grid_block(k, c):
         r0 = pl.multiple_of(k * run, run)
@@ -308,20 +314,19 @@
         vim[pl.ds(r0, run), :] = res_re * h_im + res_im * h_re
 
         def group(i, d):
-            for n in range(4):
-                regrid(k * run + 4 * i + n)
+            regrid(k * (run // 8) + i)
             return d
 
-        lax.fori_loop(0, run // 4, group, 0)
+        lax.fori_loop(0, run // 8, group, 0)
         return c
 
     lax.fori_loop(0, n_facet, grid_block, 0)
 
-    ur, uc = iota((512, 128), 0), iota((512, 128), 1)
-    unfold = jnp.where(ur // 128 == uc // 32, fold_values(uc % 32, ur % 128).astype(F32), 0.0).astype(BF16)
+    ur, uc = iota((1024, 128), 0), iota((1024, 128), 1)
+    unfold = jnp.where(ur // 256 == uc // 32, fold_values(uc % 32, ur % 32).astype(F32), 0.0).astype(BF16)
     spread = {}
     for lot in range(8):
-        moved = [jnp.dot(perm, mats[r0:r0 + 32, 8 * lot:8 * lot + 8, :].reshape(256, 128).astype(BF16),
+        moved = [jnp.dot(perm, mats[r0:r0 + 32, 8 * lot:8 * lot + 8, :].reshape(256, 256).astype(BF16),
                          preferred_element_type=F32).astype(BF16) for r0 in range(0, R, 32)]
         for m in range(8):
             part, place_x = divmod(8 * lot + m, 32)
@@ -414,7 +419,8 @@
             pltpu.VMEM((n_tile, chunk, quarter), BF16),
             pltpu.VMEM((R * 32, channels), F32),
             pltpu.VMEM((R * 32, channels), BF16),
-            pltpu.VMEM((R, 64, 128), F32),
+            pltpu.VMEM((R, 64, 256), F32),
+            pltpu.VMEM((512, channels), BF16),
             pltpu.VMEM((R, channels), F32),
             pltpu.VMEM((R, channels), F32),
             pltpu.VMEM((R, channels), F32),

time: 33 us -> 33.1 us (level)
  no operation moved by 1% of the time
where the time goes in v4:
time: 33.1 us; the launch traced here: 32.9 us
  Pallas kernels  32.3 us (98%)
  between operations  0.64 us (2%)
    pallas_call x1, Pallas kernels, local(): pl.pallas_call(body, out_shape=(jax.ShapeDtypeStruct((1, run, 2 * channel...  30.7 us
    pallas_call x1, Pallas kernels, local(): pl.pallas_call(hand_over, out_shape=(jax.ShapeDtypeStruct(resid.shape, F3...  1.57 us

profile of v4, /device:TPU:0, one launch (start us, length us, event | category | flops | bytes accessed | tf_op | source)
XLA Modules:
  0.0 32.9 jit_solution(6106354894668767493)
XLA Ops:
  0.6 30.7 %predict_regrid.1 = (f32[1,16,2048]{2,1,0:T(8,128)}, f32[1,4,2048]{2,1,0:T(4,128)}) custom-call(s32[1,2]{1,0:T(1,128)} %reader_ref.1, f32[2,2,16]{2,1,0:T(2,128)} %coords_ref.1, s32[2,16]{1,0:T(2,128)} %subgrid_ref.1, s32[2,2,16]{2,1,0:T(2,128)} %stations_ref.1, s32[2,16]{1,0:T(2,128)} %plane_ref.1, bf16[1,16,2048]{2,1,0:T(8,128)(2,1)} %rows_ref.1, ...), custom_call_target="tpu_custom_call" | custom-call | tf_op jit(solution)/shard_map/predict_regrid/pallas_call | solution.py:401
  31.3 1.6 %hand_over.1 = (f32[1,16,2048]{2,1,0:T(8,128)}, f32[1,4,2048]{2,1,0:T(4,128)}) custom-call(f32[1,16,2048]{2,1,0:T(8,128)} %get-tuple-element.4.resid_in, f32[1,4,2048]{2,1,0:T(4,128)} %get-tuple-element.5.dirty_in), custom_call_target="tpu_custom_call" | custom-call | tf_op jit(solution)/shard_map/hand_over/pallas_call | solution.py:441

commit v5 on v4

--- a/solution.py
+++ b/solution.py
@@ -48,9 +48,9 @@
     n_facet, n_tile, owned, run, channels, grid_scale,
     reader_ref, coords_ref, subgrid_ref, stations_ref, plane_ref, rows_ref, model_ref, screens_hbm, phase_ref, freq_ref,
     resid_ref, dirty_ref,
-    cols, screens, model_send, model_all, arrived, pred_send, pred_all, part_send, part_all,
+    cols, screens, model_send, model_all, arrived, pred_send, pred_all, part_sums, part_send, pair_recv, pair_send, part_all,
     te, tn, mats, weighted, hre, him, vre, vim, sre, sim,
-    local_sem, model_ss, model_rs, vis_ss, vis_rs, pred_ss, pred_rs, part_ss, part_rs,
+    local_sem, pair_ss, pair_rs, pass_ss, pass_rs, model_ss, model_rs, vis_ss, vis_rs, pred_ss, pred_rs, part_ss, part_rs,
 ):
     R = n_facet * run
     me_f = lax.axis_index("facet")
@@ -61,8 +61,13 @@
     load = pltpu.make_async_copy(screens_hbm, screens, local_sem)
     load.start()
 
-    def tile_peer(p):
-        return lax.rem(me_t + p, n_tile)
+    n_chip = n_tile // 2
+    core = lax.rem(me_t, 2)
+    chip = me_t // 2
+    sibling = me_t + 1 - 2 * core
+
+    def chip_peer(p):
+        return lax.rem(chip + p, n_chip)
 
     def facet_peer(p):
         return lax.rem(me_f + p, n_facet)
@@ -70,14 +75,15 @@
     barrier = pltpu.get_barrier_semaphore()
 
     def greet_tile(p, c):
-        pl.semaphore_signal(barrier, inc=1, device_id=(me_f, tile_peer(p)), device_id_type=MESH)
+        pl.semaphore_signal(barrier, inc=1, device_id=(me_f, 2 * chip_peer(p) + core), device_id_type=MESH)
         return c
 
     def greet_facet(p, c):
         pl.semaphore_signal(barrier, inc=1, device_id=(facet_peer(p), me_t), device_id_type=MESH)
         return c
 
-    lax.fori_loop(1, n_tile, greet_tile, 0)
+    pl.semaphore_signal(barrier, inc=1, device_id=(me_f, sibling), device_id_type=MESH)
+    lax.fori_loop(1, n_chip, greet_tile, 0)
     lax.fori_loop(1, n_facet, greet_facet, 0)
 
     model_f = model_ref[0].astype(F32)
@@ -119,13 +125,22 @@
 
         lax.fori_loop(0, R // 8, group, 0)
 
-    tables(0, te)
-    pl.semaphore_wait(barrier, n_tile + n_facet - 2)
-
-    def model_copy(o, slot):
+    pl.semaphore_wait(barrier, n_chip + n_facet - 1)
+
+    def model_copy(o, origin):
         return pltpu.make_async_remote_copy(
-            src_ref=model_send, dst_ref=model_all.at[slot], send_sem=model_ss.at[o],
-            recv_sem=model_rs.at[slot], device_id=(me_f, o), device_id_type=MESH)
+            src_ref=model_send, dst_ref=model_all.at[2 * origin + core], send_sem=model_ss.at[o],
+            recv_sem=model_rs.at[origin], device_id=(me_f, 2 * o + core), device_id_type=MESH)
+
+    def forward(o):
+        return pltpu.make_async_remote_copy(
+            src_ref=model_all.at[2 * o + core], dst_ref=model_all.at[2 * o + core], send_sem=pass_ss.at[o],
+            recv_sem=pass_rs.at[o], device_id=(me_f, sibling), device_id_type=MESH)
+
+    def passed(o):
+        return pltpu.make_async_remote_copy(
+            src_ref=model_all.at[2 * o + core], dst_ref=model_all.at[2 * o + 1 - core], send_sem=pass_ss.at[o],
+            recv_sem=pass_rs.at[o], device_id=(me_f, sibling), device_id_type=MESH)
 
     def vis_copy(o, slot):
         return pltpu.make_async_remote_copy(
@@ -137,25 +152,35 @@
             src_ref=pred_send.at[k], dst_ref=pred_all.at[slot, k], send_sem=pred_ss.at[o, k],
             recv_sem=pred_rs.at[slot, k], device_id=(o, me_t), device_id_type=MESH)
 
-    def part_copy(o, slot):
+    def part_copy(o, origin):
         return pltpu.make_async_remote_copy(
-            src_ref=part_send.at[o], dst_ref=part_all.at[slot], send_sem=part_ss.at[o],
-            recv_sem=part_rs.at[slot], device_id=(me_f, o), device_id_type=MESH)
+            src_ref=pair_send.at[o], dst_ref=part_all.at[origin], send_sem=part_ss.at[o],
+            recv_sem=part_rs.at[origin], device_id=(me_f, 2 * o + core), device_id_type=MESH)
 
     def send_model(p, c):
-        model_copy(tile_peer(p), me_t).start()
+        model_copy(chip_peer(p), chip).start()
         return c
 
     def send_vis(p, c):
         vis_copy(facet_peer(p), me_f).start()
         return c
 
-    lax.fori_loop(1, n_tile, send_model, 0)
+    lax.fori_loop(1, n_chip, send_model, 0)
     lax.fori_loop(1, n_facet, send_vis, 0)
     model_all[me_t] = model_send[...]
+    forward(chip).start()
     arrived[me_f] = rows_ref[0]
 
+    tables(0, te)
     tables(1, tn)
+
+    def pass_on(p, c):
+        o = chip_peer(p)
+        model_copy(o, o).wait()
+        forward(o).start()
+        return c
+
+    lax.fori_loop(1, n_chip, pass_on, 0)
 
     stations = screens.shape[0]
     planes, pixels = phase_ref.shape
@@ -175,12 +200,11 @@
     sre[...] = pair_re * wave_re - pair_im * wave_im
     sim[...] = pair_re * wave_im + pair_im * wave_re
 
-    def wait_model(p, c):
-        o = tile_peer(p)
-        model_copy(o, o).wait()
-        return c
-
-    lax.fori_loop(1, n_tile, wait_model, 0)
+    def wait_passed(p, c):
+        passed(chip_peer(p)).wait()
+        return c
+
+    lax.fori_loop(0, n_chip, wait_passed, 0)
     total = n_tile * chunk
     own_i = iota((4 * R, total), 1)
     sub_col = jnp.concatenate([column([subgrid_ref[k:k + 1, :] for k in range(n_facet)])] * 4, axis=0)
@@ -347,23 +371,33 @@
     own_r = iota((total, 4 * R), 0)
     sub_row = jnp.sum(
         jnp.where(iota((4 * R, 4 * R), 0) == iota((4 * R, 4 * R), 1), sub_col, 0.0), axis=0, keepdims=True)
-    place = (sub_row == ((own_r // chunk) * owned + own_r % owned).astype(F32)) & (
+    goal = own_r // chunk % n_chip * 2 + own_r // chunk // n_chip
+    place = (sub_row == (goal * owned + own_r % owned).astype(F32)) & (
         (own_r // owned) % 4 == iota((total, 4 * R), 1) // R)
     sums = jnp.dot(place.astype(F32).astype(BF16), stacked, preferred_element_type=F32)
-    part_send[...] = sums.astype(BF16).reshape(n_tile, chunk, quarter)
+    sums = sums.reshape(n_tile, chunk, quarter)
+    part_sums[...] = sums
+    part_send[...] = sums.astype(BF16)
+    pair_copy = pltpu.make_async_remote_copy(
+        src_ref=part_send.at[pl.ds((1 - core) * n_chip, n_chip)], dst_ref=pair_recv, send_sem=pair_ss,
+        recv_sem=pair_rs, device_id=(me_f, sibling), device_id_type=MESH)
+    pair_copy.start()
+    pair_copy.wait()
+    pair_send[...] = (part_sums[pl.ds(core * n_chip, n_chip)] + pair_recv[...].astype(F32)).astype(BF16)
 
     def send_part(p, c):
-        part_copy(tile_peer(p), me_t).start()
-        return c
-
-    lax.fori_loop(1, n_tile, send_part, 0)
+        part_copy(chip_peer(p), chip).start()
+        return c
+
+    lax.fori_loop(1, n_chip, send_part, 0)
 
     def add_part(p, acc):
-        o = tile_peer(p)
+        o = chip_peer(p)
         part_copy(o, o).wait()
         return acc + part_all[o].astype(F32)
 
-    acc = lax.fori_loop(1, n_tile, add_part, part_send[me_t].astype(F32))
+    own = part_sums[core * n_chip + chip] + pair_recv[chip].astype(F32)
+    acc = lax.fori_loop(1, n_chip, add_part, own)
     for q in range(4):
         dirty_ref[0, :, q * quarter:(q + 1) * quarter] = acc[q * owned:(q + 1) * owned]
 
@@ -415,8 +449,11 @@
             pltpu.VMEM((n_facet, run, 2 * channels), BF16),
             pltpu.VMEM((n_facet, run, 2 * channels), BF16),
             pltpu.VMEM((n_facet, n_facet, run, 2 * channels), BF16),
+            pltpu.VMEM((n_tile, chunk, quarter), F32),
             pltpu.VMEM((n_tile, chunk, quarter), BF16),
-            pltpu.VMEM((n_tile, chunk, quarter), BF16),
+            pltpu.VMEM((n_tile // 2, chunk, quarter), BF16),
+            pltpu.VMEM((n_tile // 2, chunk, quarter), BF16),
+            pltpu.VMEM((n_tile // 2, chunk, quarter), BF16),
             pltpu.VMEM((R * 32, channels), F32),
             pltpu.VMEM((R * 32, channels), BF16),
             pltpu.VMEM((R, 64, 256), F32),
@@ -427,11 +464,12 @@
             pltpu.VMEM((R, channels), F32),
             pltpu.VMEM((R, pixels), F32),
             pltpu.VMEM((R, pixels), F32),
-            dma,
-            dma((n_tile,)), dma((n_tile,)),
+            dma, dma, dma,
+            dma((n_tile // 2,)), dma((n_tile // 2,)),
+            dma((n_tile // 2,)), dma((n_tile // 2,)),
             dma((n_facet,)), dma((n_facet,)),
             dma((n_facet, n_facet)), dma((n_facet, n_facet)),
-            dma((n_tile,)), dma((n_tile,)),
+            dma((n_tile // 2,)), dma((n_tile // 2,)),
         ],
         compiler_params=pltpu.CompilerParams(
             collective_id=0, has_side_effects=True, vmem_limit_bytes=60 * 1024 * 1024),

time: 33.1 us -> 32.1 us (0.970)
  Pallas kernels: 32.3 us -> 31.3 us
    pallas_call x1, Pallas kernels: 30.7 us -> 29.8 us  [local(): pl.pallas_call(body, out_shape=(jax.ShapeDtypeStruct((1, run, 2 * channel...]
where the time goes in v5:
time: 32.1 us; the launch traced here: 32 us
  Pallas kernels  31.3 us (98%)
  between operations  0.64 us (2%)
    pallas_call x1, Pallas kernels, local(): pl.pallas_call(body, out_shape=(jax.ShapeDtypeStruct((1, run, 2 * channel...  29.8 us
    pallas_call x1, Pallas kernels, local(): pl.pallas_call(hand_over, out_shape=(jax.ShapeDtypeStruct(resid.shape, F3...  1.57 us

profile of v5, /device:TPU:0, one launch (start us, length us, event | category | flops | bytes accessed | tf_op | source)
XLA Modules:
  0.0 32.0 jit_solution(11617152635470774766)
XLA Ops:
  0.6 29.8 %predict_regrid.1 = (f32[1,16,2048]{2,1,0:T(8,128)}, f32[1,4,2048]{2,1,0:T(4,128)}) custom-call(s32[1,2]{1,0:T(1,128)} %reader_ref.1, f32[2,2,16]{2,1,0:T(2,128)} %coords_ref.1, s32[2,16]{1,0:T(2,128)} %subgrid_ref.1, s32[2,2,16]{2,1,0:T(2,128)} %stations_ref.1, s32[2,16]{1,0:T(2,128)} %plane_ref.1, bf16[1,16,2048]{2,1,0:T(8,128)(2,1)} %rows_ref.1, ...), custom_call_target="tpu_custom_call" | custom-call | tf_op jit(solution)/shard_map/predict_regrid/pallas_call | solution.py:435
  30.4 1.6 %hand_over.1 = (f32[1,16,2048]{2,1,0:T(8,128)}, f32[1,4,2048]{2,1,0:T(4,128)}) custom-call(f32[1,16,2048]{2,1,0:T(8,128)} %get-tuple-element.4.resid_in, f32[1,4,2048]{2,1,0:T(4,128)} %get-tuple-element.5.dirty_in), custom_call_target="tpu_custom_call" | custom-call | tf_op jit(solution)/shard_map/hand_over/pallas_call | solution.py:479

commit v6 on v5

--- a/solution.py
+++ b/solution.py
@@ -123,7 +123,7 @@
                     him[pl.ds(r0, 8), lanes] = ca * s0 + sa * c0
             return c
 
-        lax.fori_loop(0, R // 8, group, 0)
+        lax.fori_loop(0, R // 8, group, 0, unroll=2)
 
     pl.semaphore_wait(barrier, n_chip + n_facet - 1)
 
@@ -259,7 +259,7 @@
             degrid(k * (run // 8) + i)
             return d
 
-        lax.fori_loop(0, run // 8, group, 0)
+        lax.fori_loop(0, run // 8, group, 0, unroll=2)
         r0 = pl.multiple_of(k * run, run)
         a_re, a_im = vre[pl.ds(r0, run), :], vim[pl.ds(r0, run), :]
         h_re, h_im = hre[pl.ds(r0, run), :], him[pl.ds(r0, run), :]
@@ -341,7 +341,7 @@
             regrid(k * (run // 8) + i)
             return d
 
-        lax.fori_loop(0, run // 8, group, 0)
+        lax.fori_loop(0, run // 8, group, 0, unroll=2)
         return c
 
     lax.fori_loop(0, n_facet, grid_block, 0)

time: 32.1 us -> 31.6 us (0.984)
  Pallas kernels: 31.3 us -> 30.8 us
    pallas_call x1, Pallas kernels: 29.8 us -> 29.2 us  [local(): pl.pallas_call(body, out_shape=(jax.ShapeDtypeStruct((1, run, 2 * channel...]
where the time goes in v6:
time: 31.6 us; the launch traced here: 31.5 us
  Pallas kernels  30.8 us (97%)
  between operations  0.64 us (2%)
    pallas_call x1, Pallas kernels, local(): pl.pallas_call(body, out_shape=(jax.ShapeDtypeStruct((1, run, 2 * channel...  29.2 us
    pallas_call x1, Pallas kernels, local(): pl.pallas_call(hand_over, out_shape=(jax.ShapeDtypeStruct(resid.shape, F3...  1.57 us

profile of v6, /device:TPU:0, one launch (start us, length us, event | category | flops | bytes accessed | tf_op | source)
XLA Modules:
  0.0 31.5 jit_solution(10745436455803872637)
XLA Ops:
  0.6 29.2 %predict_regrid.1 = (f32[1,16,2048]{2,1,0:T(8,128)}, f32[1,4,2048]{2,1,0:T(4,128)}) custom-call(s32[1,2]{1,0:T(1,128)} %reader_ref.1, f32[2,2,16]{2,1,0:T(2,128)} %coords_ref.1, s32[2,16]{1,0:T(2,128)} %subgrid_ref.1, s32[2,2,16]{2,1,0:T(2,128)} %stations_ref.1, s32[2,16]{1,0:T(2,128)} %plane_ref.1, bf16[1,16,2048]{2,1,0:T(8,128)(2,1)} %rows_ref.1, ...), custom_call_target="tpu_custom_call" | custom-call | tf_op jit(solution)/shard_map/predict_regrid/pallas_call | solution.py:435
  29.9 1.6 %hand_over.1 = (f32[1,16,2048]{2,1,0:T(8,128)}, f32[1,4,2048]{2,1,0:T(4,128)}) custom-call(f32[1,16,2048]{2,1,0:T(8,128)} %get-tuple-element.4.resid_in, f32[1,4,2048]{2,1,0:T(4,128)} %get-tuple-element.5.dirty_in), custom_call_target="tpu_custom_call" | custom-call | tf_op jit(solution)/shard_map/hand_over/pallas_call | solution.py:479
